TPU v7x, 1024 devices: a whole 4x8x16 slice. The times are simulated.
1024 devices in a mesh: dp: 16 (over y, z_hi), tensor: 64 (over x, z_lo, core).
Axes of the slice: x: 4, y: 8, z: 16 (z_hi: 2, z_lo: 8; z = z_hi * 8 + z_lo), core: 2. Of those that a mesh axis runs over, the one named last changes fastest.
Arguments:
- gate_input: bfloat16 [2048, 16384], P('dp', 'tensor'), may hold values from -6 to 6
- up_input: bfloat16 [2048, 16384], P('dp', 'tensor'), may hold values from -6 to 6
- residual: bfloat16 [2048, 4096], P('dp', 'tensor'), may hold values from -6 to 6
- down_proj: bfloat16 [16384, 4096], P('tensor', 'dp'), may hold values from -0.125 to 0.125
- cotangent: bfloat16 [2048, 4096], P('dp', 'tensor'), may hold values from -16 to 16
Outputs:
- layer_out: bfloat16 [2048, 4096], P('dp', 'tensor')
- gate_grad: bfloat16 [2048, 16384], P('dp', 'tensor')
- up_grad: bfloat16 [2048, 16384], P('dp', 'tensor')
- down_grad: bfloat16 [16384, 4096], P('tensor', 'dp')
All inputs are finite; a program needn't handle non-finite values.
Results may differ from a plain program's by a relative error of at most 0.02.
Values may be sent and summed in bfloat16 or wider, within the bound.
No kernel may reach another device: no remote copies, remote signals or barrier semaphores. Data moves between devices by JAX's collectives and lax.ppermute only.
A program may use at most 32 MiB of HBM per device.

v0:
```python
import math

import jax
import jax.numpy as jnp
from jax import lax
from jax.sharding import PartitionSpec as P


def body(gate_input, up_input, residual, down_proj, cotangent):
    tok_rows = gate_input.shape[0]
    groups = lax.axis_size("dp")
    norm_factor = 1.0 / math.sqrt(tok_rows * groups)
    full_weights = lax.all_gather(down_proj, "dp", axis=1, tiled=True)
    gate_values = gate_input.astype(jnp.float32)
    up_values = up_input.astype(jnp.float32)
    sigmoid_gate = jax.nn.sigmoid(gate_values)
    hidden = (gate_values * sigmoid_gate * up_values).astype(jnp.bfloat16)
    projected = jnp.dot(hidden, full_weights, preferred_element_type=jnp.float32)
    summed = lax.psum_scatter(projected, "tensor", scatter_dimension=1, tiled=True)
    layer_out = (residual.astype(jnp.float32) + summed).astype(jnp.bfloat16)
    cot_full = lax.all_gather(cotangent, "tensor", axis=1, tiled=True)
    hidden_grad = lax.dot_general(
        cot_full, full_weights, (((1,), (1,)), ((), ())), preferred_element_type=jnp.float32
    )
    up_grad = (hidden_grad * gate_values * sigmoid_gate).astype(jnp.bfloat16)
    gate_grad = (
        hidden_grad * up_values * sigmoid_gate * (1.0 + gate_values * (1.0 - sigmoid_gate))
    ).astype(jnp.bfloat16)
    local_term = lax.dot_general(
        hidden, cot_full, (((0,), (0,)), ((), ())), preferred_element_type=jnp.float32
    )
    running = lax.psum_scatter(
        local_term.astype(jnp.bfloat16), "dp", scatter_dimension=1, tiled=True
    ).astype(jnp.float32)
    down_grad = (running * norm_factor).astype(jnp.bfloat16)
    return (layer_out, gate_grad, up_grad, down_grad)


def solution(mesh):
    in_specs = (
        P("dp", "tensor"),
        P("dp", "tensor"),
        P("dp", "tensor"),
        P("tensor", "dp"),
        P("dp", "tensor"),
    )
    out_specs = (P("dp", "tensor"), P("dp", "tensor"), P("dp", "tensor"), P("tensor", "dp"))
    return jax.shard_map(body, mesh=mesh, in_specs=in_specs, out_specs=out_specs, check_vma=False)
```

profile of v0, /device:TPU:48, one launch (start us, length us, event | category | flops | bytes accessed | tf_op | source)
XLA Modules:
  0.0 996.4 jit_solution(15872081829245532774)
XLA Ops:
  7.2 0.0 all-gather.5.cloned.1.call-start
  7.2 0.7 all-gather.5.cloned.1.call-update
  7.9 0.0 all-gather.3.cloned.1.call-start
  7.9 0.7 all-gather.3.cloned.1.call-update
  8.6 0.0 copy-start.2
  8.7 0.0 copy-start.3
  8.7 0.0 reduce-scatter.5.cloned.1.call-start
  8.7 132.2 %all-gather.5.cloned.1.call-done = bf16[128,4096]{0,1:T(8,128)(2,1)} async-done(((bf16[128,64]{0,1:T(8,128)(2,1)}), bf16[128,4096]{0,1:T(8,128)(2,1)}) %all-gather.5.cloned.1.call-update) | async-done | bytes 1048592 | tf_op jit(solution)/shard_map/all_gather | solution.py:21
  140.9 3.4 convolution_convert_fusion
  144.3 0.0 reduce-scatter.5.cloned.1.call-update
  144.3 0.0 reduce-scatter.3.cloned.1.call-start
  144.3 142.7 %all-gather.3.cloned.1.call-done = bf16[256,4096]{1,0:T(8,128)(2,1)} async-done(((bf16[256,256]{1,0:T(8,128)(2,1)}), bf16[256,4096]{1,0:T(8,128)(2,1)}) %all-gather.3.cloned.1.call-update) | async-done | bytes 2097168 | tf_op jit(solution)/shard_map/all_gather | solution.py:13
  287.1 0.0 copy-done.2
  287.1 0.0 copy-done.3
  287.1 0.0 copy-start.1
  287.1 4.0 fusion.11
  291.0 0.0 copy-start
  291.0 0.0 reduce-scatter.3.cloned.1.call-update
  291.1 0.0 copy-done.1
  291.1 1.6 copy-done
  292.6 0.0 copy-start.4
  292.6 1.5 fusion.9
  294.1 256.6 %reduce-scatter.5.cloned.1.call-done = bf16[256,256]{1,0:T(8,128)(2,1)} async-done(((bf16[256,4096]{1,0:T(8,128)(2,1)}), bf16[256,256]{1,0:T(8,128)(2,1)}) %reduce-scatter.5.cloned.1.call-update) | async-done | bytes 131088 | tf_op jit(solution)/shard_map/reduce_scatter | solution.py:32
  550.8 1.6 multiply_convert_fusion
  552.4 436.2 %reduce-scatter.3.cloned.1.call-done = f32[128,64]{0,1:T(8,128)} async-done(((f32[128,4096]{0,1:T(8,128)}), f32[128,64]{0,1:T(8,128)}) %reduce-scatter.3.cloned.1.call-update) | async-done | bytes 32784 | tf_op jit(solution)/shard_map/reduce_scatter | solution.py:19
  988.5 0.0 copy-done.4
  988.5 1.4 add_convert_fusion
Async XLA Ops:
  7.2 133.7 %all-gather.5.cloned.1.call-start = ((), (), s32[]{:S(2)}) async-start(), calls=%async_computation.4 | async-start | bytes 1064960 | tf_op jit(solution)/shard_map/all_gather | solution.py:21
  7.9 279.2 %all-gather.3.cloned.1.call-start = ((), (), s32[]{:S(2)}) async-start(), calls=%async_computation.2 | async-start | bytes 2228224 | tf_op jit(solution)/shard_map/all_gather | solution.py:13
  8.6 278.4 %copy-start.2 = (bf16[128,256]{1,0:T(8,128)(2,1)S(1)}, bf16[128,256]{1,0:T(8,128)(2,1)}, u32[]{:S(2)}) copy-start(bf16[128,256]{1,0:T(8,128)(2,1)} %param.6) | copy-start | bytes 196612
  8.7 278.4 %copy-start.3 = (bf16[128,256]{1,0:T(8,128)(2,1)S(1)}, bf16[128,256]{1,0:T(8,128)(2,1)}, u32[]{:S(2)}) copy-start(bf16[128,256]{1,0:T(8,128)(2,1)} %param.5) | copy-start | bytes 196612
  8.7 542.1 %reduce-scatter.5.cloned.1.call-start = ((), (), s32[]{:S(2)}) async-start(), calls=%async_computation.5 | async-start | bytes 2228224 | tf_op jit(solution)/shard_map/reduce_scatter | solution.py:32
  144.3 844.2 %reduce-scatter.3.cloned.1.call-start = ((), (), s32[]{:S(2)}) async-start(), calls=%async_computation.3 | async-start | bytes 2129920 | tf_op jit(solution)/shard_map/reduce_scatter | solution.py:19
  287.1 4.0 copy-start.1
  291.0 1.6 copy-start
  292.6 695.9 %copy-start.4 = (bf16[128,64]{0,1:T(8,128)(2,1)S(1)}, bf16[128,64]{0,1:T(8,128)(2,1)}, u32[]{:S(2)}) copy-start(bf16[128,64]{0,1:T(8,128)(2,1)} %param.7) | copy-start | bytes 49156
Sparse Core Ops, SparseCore 0:
  10.7 130.1 all-gather.4
  145.1 141.9 all-gather.2
  292.8 257.9 reduce-scatter.4
  554.4 434.1 reduce-scatter.2
where the time goes:
time: 997 us; the launch traced here: 996 us
  waiting for transfers between devices  969 us (97%)
  between operations  13.8 us (1%)
    reduce_scatter x1, waiting for transfers between devices, body(): lax.psum_scatter(projected, 'tensor', scatter_dimension=1, tiled=True)  436 us
    reduce_scatter x1, waiting for transfers between devices, body(): lax.psum_scatter(local_term.astype(jnp.bfloat16), 'dp', scatter_dimension...  257 us
    all_gather x1, waiting for transfers between devices, body(): full_weights = lax.all_gather(down_proj, 'dp', axis=1, tiled=True)  143 us
    all_gather x1, waiting for transfers between devices, body(): cot_full = lax.all_gather(cotangent, 'tensor', axis=1, tiled=True)  132 us
  transfers between devices with their start and end apart: 4, of which 4 were waited for; matrix products, arithmetic and copies ran while one was open for 1% of the time, Pallas kernels for 0%

commit v1 on v0

v1 whole, which is shorter than its diff:
```python
import math

import jax
import jax.numpy as jnp
from jax import lax
from jax.sharding import Mesh
from jax.sharding import PartitionSpec as P

AXES = ("y", "zh", "x", "zl", "c")
SIZES = (8, 2, 4, 8, 2)
BF, F32 = jnp.bfloat16, jnp.float32


def swap_pairs():
    def at(y, zh, x, zl, c):
        return (((y * 2 + zh) * 4 + x) * 8 + zl) * 2 + c

    return [
        (at(y, zh, x, zl, c), at(2 * x + zl // 4, zh, y // 2, 4 * (y % 2) + zl % 4, c))
        for y in range(8)
        for zh in range(2)
        for x in range(4)
        for zl in range(8)
        for c in range(2)
    ]


def gather(part, axis):
    return lax.all_to_all(jnp.broadcast_to(part[None], (lax.axis_size(axis),) + part.shape), axis, 0, 0)


def scatter_sum(parts, axis):
    return jnp.sum(lax.all_to_all(parts, axis, 0, 0).astype(F32), axis=0)


def body(gate_input, up_input, residual, down_proj, cotangent):
    swap = swap_pairs()
    zh = lax.axis_index("zh")
    across = [(0, 1), (1, 0)]
    weights_other = lax.ppermute(down_proj, "zh", across)
    cot_moved = lax.ppermute(cotangent.T, AXES, swap)

    gate = gate_input.astype(F32)
    up = up_input.astype(F32)
    sig = jax.nn.sigmoid(gate)
    hidden = (gate * sig * up).astype(BF)

    hid = gather(hidden, "y")
    cot = gather(gather(gather(cot_moved, "zl"), "x"), "c")
    cot = cot.reshape(2, 4, 2, 4, 64, 128)

    low = jnp.where(zh == 0, down_proj, weights_other)
    high = jnp.where(zh == 0, weights_other, down_proj)
    weights = jnp.concatenate([low, high], axis=1).reshape(256, 4, 2, 64)

    proj = jnp.einsum(
        "klcf,xhtk->cxhlft", weights, hid.reshape(4, 2, 128, 256), preferred_element_type=F32
    ).astype(BF)
    proj = scatter_sum(proj, "c").astype(BF)
    proj = scatter_sum(proj, "x").astype(BF)
    proj = scatter_sum(proj.reshape(8, 64, 128), "zl")
    proj = lax.ppermute(proj, AXES, swap)
    layer_out = (residual.astype(F32).T + proj).astype(BF).T

    cot_rows = jnp.transpose(cot, (3, 0, 4, 1, 2, 5)).reshape(512, 1024)
    partial = lax.dot_general(
        cot_rows, weights.reshape(256, 512), (((0,), (1,)), ((), ())), preferred_element_type=F32
    ).astype(BF)
    hidden_grad = scatter_sum(partial.reshape(8, 128, 256), "y")
    up_grad = (hidden_grad * gate * sig).astype(BF)
    gate_grad = (hidden_grad * up * sig * (1.0 + gate * (1.0 - sig))).astype(BF)

    hid_rows = hid.reshape(1024, 256)

    def term(which):
        feats = lax.dynamic_slice_in_dim(cot_rows, which * 256, 256, 0)
        return lax.dot_general(hid_rows, feats, (((0,), (1,)), ((), ())), preferred_element_type=F32)

    arrived = lax.ppermute(term(1 - zh).astype(BF), "zh", across)
    down_grad = ((term(zh) + arrived.astype(F32)) * (1.0 / math.sqrt(2048))).astype(BF)
    return (layer_out, gate_grad, up_grad, down_grad)


def solution(mesh):
    fine = Mesh(mesh.devices.reshape(SIZES), AXES)
    dp, tensor = ("y", "zh"), ("x", "zl", "c")
    in_specs = (P(dp, tensor), P(dp, tensor), P(dp, tensor), P(tensor, dp), P(dp, tensor))
    out_specs = (P(dp, tensor), P(dp, tensor), P(dp, tensor), P(tensor, dp))
    return jax.shard_map(body, mesh=fine, in_specs=in_specs, out_specs=out_specs, check_vma=False)
```

time: 997 us -> 179 us (0.18)
  the two profiles are of different devices: /device:TPU:48 before, /device:TPU:9 now
where the time goes in v1:
time: 179 us; the launch traced here: 178 us
  starting transfers between devices  73.6 us (41%)
  blocking collectives  49.7 us (28%)
  waiting for transfers between devices  43.3 us (24%)
  local copies, waits for them, and re-layouts  6.85 us (4%)
  matrix products  2.26 us (1%)
  other arithmetic  1.85 us (1%)
    all_to_all x2, blocking collectives, gather(): lax.all_to_all(jnp.broadcast_to(part[None], (lax.axis_size(axis),) + part...  31.2 us
    all_to_all x2, blocking collectives, scatter_sum(): return jnp.sum(lax.all_to_all(parts, axis, 0, 0).astype(F32), axis=0)  18.5 us
    all_to_all x2, starting transfers between devices, gather(): lax.all_to_all(jnp.broadcast_to(part[None], (lax.axis_size(axis),) + part...  17.4 us
    all_to_all x2, waiting for transfers between devices, gather(): lax.all_to_all(jnp.broadcast_to(part[None], (lax.axis_size(axis),) + part...  15.6 us
    all_to_all x2, waiting for transfers between devices, scatter_sum(): return jnp.sum(lax.all_to_all(parts, axis, 0, 0).astype(F32), axis=0)  15.2 us
    all_to_all x2, starting transfers between devices, scatter_sum(): return jnp.sum(lax.all_to_all(parts, axis, 0, 0).astype(F32), axis=0)  13.8 us
    ppermute x1, starting transfers between devices, body(): weights_other = lax.ppermute(down_proj, 'zh', across)  11.8 us
    ppermute x1, starting transfers between devices, body(): arrived = lax.ppermute(term(1 - zh).astype(BF), 'zh', across)  11.7 us
  transfers between devices with their start and end apart: 8, of which 5 were waited for; matrix products, arithmetic and copies ran while one was open for 2% of the time, Pallas kernels for 0%

profile of v1, /device:TPU:9, one launch (start us, length us, event | category | flops | bytes accessed | tf_op | source)
XLA Modules:
  0.0 178.4 jit_solution(9495699288898273237)
XLA Ops:
  0.6 0.0 copy-start
  0.6 10.7 %collective-permute-start.2 = (bf16[64,128]{1,0:T(8,128)(2,1)}, bf16[64,128]{1,0:T(8,128)(2,1)S(1)}, u32[]{:S(2)}, u32[]{:S(2)}) collective-permute-start(bf16[64,128]{1,0:T(8,128)(2,1)} %bitcast.42), channel_id=1, source_target_pairs={{0,0},{1,1},{2,2},{3,3},{4,4},{5,5},{6,6},{7,7},{8,128},{9,129},{1... | collective-permute-start | bytes 49160 | tf_op jit(solution)/shard_map/ppermute | solution.py:41
  11.3 1.3 collective-permute-done.2
  12.6 17.2 %all_to_all.40 = bf16[8,64,128]{2,1,0:T(8,128)(2,1)S(1)} all-to-all(bf16[8,64,128]{2,1,0:T(8,128)(2,1)S(1)} %broadcast_in_dim.9), channel_id=1, replica_groups=mesh['y'=8,'zh'=2,'x'=4,'zl'=8,'c'=2] {'zl'}, dimensions={0} | all-to-all | bytes 262144 | tf_op jit(solution)/shard_map/all_to_all | solution.py:29
  29.8 0.9 broadcast_in_dim.10
  30.7 11.6 %all-to-all-start.5 = ((bf16[4,8,64,128]{3,2,1,0:T(8,128)(2,1)}), bf16[4,8,64,128]{3,2,1,0:T(8,128)(2,1)S(1)}, u32[]{:S(2)}, u32[]{:S(2)}) async-start(bf16[4,8,64,128]{3,2,1,0:T(8,128)(2,1)} %broadcast_in_dim.10), calls=%async_computation.5 | async-start | bytes 1048576 | tf_op jit(solution)/shard_map/all_to_all | solution.py:29
  42.3 0.0 copy-done
  42.3 11.8 %collective-permute-start = (bf16[256,256]{1,0:T(8,128)(2,1)S(1)}, bf16[256,256]{1,0:T(8,128)(2,1)S(1)}, u32[]{:S(2)}, u32[]{:S(2)}) collective-permute-start(bf16[256,256]{1,0:T(8,128)(2,1)S(1)} %copy-done), channel_id=1, source_target_pairs={{0,64},{64,0},{1,65},{65,1},{2,66},{66,2},{3,67},{67,3},{4,68},{68... | collective-permute-start | bytes 393224 | tf_op jit(solution)/shard_map/ppermute | solution.py:40
  54.1 2.7 %collective-permute-done = bf16[256,256]{1,0:T(8,128)(2,1)S(1)} collective-permute-done((bf16[256,256]{1,0:T(8,128)(2,1)S(1)}, bf16[256,256]{1,0:T(8,128)(2,1)S(1)}, u32[]{:S(2)}, u32[]{:S(2)}) %collective-permute-start) | collective-permute-done | bytes 131104 | tf_op jit(solution)/shard_map/ppermute | solution.py:40
  56.8 0.0 all-to-all-done.5
  56.8 0.3 broadcast_in_dim.11
  57.1 14.1 %all_to_all.41 = bf16[2,4,8,64,128]{4,3,2,1,0:T(8,128)(2,1)S(1)} all-to-all(bf16[2,4,8,64,128]{4,3,2,1,0:T(8,128)(2,1)S(1)} %broadcast_in_dim.11), channel_id=1, replica_groups=mesh['y'=8,'zh'=2,'x'=4,'zl'=8,'c'=2] {'c'}, dimensions={0} | all-to-all | bytes 2097152 | tf_op jit(solution)/shard_map/all_to_all | solution.py:29
  71.2 1.1 copy.28
  72.3 0.8 reshape.37
  73.1 0.4 fusion.1
  73.5 0.0 copy-start.1
  73.5 0.0 copy-start.2
  73.5 0.9 copy.38
  74.4 10.0 %all-to-all-start.7 = ((bf16[8,128,256]{1,2,0:T(8,128)(2,1)}), bf16[8,128,256]{1,2,0:T(8,128)(2,1)S(1)}, u32[]{:S(2)}, u32[]{:S(2)}) async-start(bf16[8,128,256]{1,2,0:T(8,128)(2,1)} %bitcast.36), calls=%async_computation.7 | async-start | bytes 1048576 | tf_op jit(solution)/shard_map/all_to_all | solution.py:33
  84.4 0.0 copy-done.1
  84.4 0.1 copy.23
  84.6 0.1 copy.24
  84.7 15.2 %all-to-all-done.7 = bf16[8,128,256]{1,2,0:T(8,128)(2,1)S(1)} async-done(((bf16[8,128,256]{1,2,0:T(8,128)(2,1)}), bf16[8,128,256]{1,2,0:T(8,128)(2,1)S(1)}, u32[]{:S(2)}, u32[]{:S(2)}) %all-to-all-start.7) | async-done | bytes 524320 | tf_op jit(solution)/shard_map/all_to_all | solution.py:33
  99.9 0.1 convert_reduce_fusion
  100.0 0.1 fusion.14
  100.1 0.1 copy.25
  100.2 0.8 broadcast_in_dim.8
  101.0 5.9 %all-to-all-start = ((bf16[8,128,256]{2,1,0:T(8,128)(2,1)}), bf16[8,128,256]{2,1,0:T(8,128)(2,1)S(1)}, u32[]{:S(2)}, u32[]{:S(2)}) async-start(bf16[8,128,256]{2,1,0:T(8,128)(2,1)} %broadcast_in_dim.8), calls=%async_computation | async-start | bytes 1048576 | tf_op jit(solution)/shard_map/all_to_all | solution.py:29
  106.9 0.1 copy.26
  107.1 15.6 %all-to-all-done = bf16[8,128,256]{2,1,0:T(8,128)(2,1)S(1)} async-done(((bf16[8,128,256]{2,1,0:T(8,128)(2,1)}), bf16[8,128,256]{2,1,0:T(8,128)(2,1)S(1)}, u32[]{:S(2)}, u32[]{:S(2)}) %all-to-all-start) | async-done | bytes 524320 | tf_op jit(solution)/shard_map/all_to_all | solution.py:29
  122.7 0.5 fusion
  123.2 0.1 copy.27
  123.3 5.7 %all_to_all.42 = bf16[2,4,2,4,64,128]{5,4,3,2,1,0:T(8,128)(2,1)S(1)} all-to-all(bf16[2,4,2,4,64,128]{5,4,3,2,1,0:T(8,128)(2,1)S(1)} %copy.27), channel_id=1, replica_groups=mesh['y'=8,'zh'=2,'x'=4,'zl'=8,'c'=2] {'c'}, dimensions={0} | all-to-all | bytes 2097152 | tf_op jit(solution)/shard_map/all_to_all | solution.py:33
  129.0 0.3 reduce_sum.42
  129.2 12.8 %all_to_all.43 = bf16[4,2,4,64,128]{4,3,2,1,0:T(8,128)(2,1)S(1)} all-to-all(bf16[4,2,4,64,128]{4,3,2,1,0:T(8,128)(2,1)S(1)} %reduce_sum.42), channel_id=1, replica_groups=mesh['y'=8,'zh'=2,'x'=4,'zl'=8,'c'=2] {'x'}, dimensions={0} | all-to-all | bytes 1048576 | tf_op jit(solution)/shard_map/all_to_all | solution.py:33
  142.0 0.7 reduce_sum.43
  142.8 3.8 %all-to-all-start.3 = ((bf16[8,64,128]{2,1,0:T(8,128)(2,1)}), bf16[8,64,128]{2,1,0:T(8,128)(2,1)S(1)}, u32[]{:S(2)}, u32[]{:S(2)}) async-start(bf16[8,64,128]{2,1,0:T(8,128)(2,1)} %bitcast.8), calls=%async_computation.3 | async-start | bytes 262144 | tf_op jit(solution)/shard_map/all_to_all | solution.py:33
  146.5 0.3 convolution_convert_fusion.2
  146.9 0.0 copy-start.3
  146.9 11.7 %collective-permute-start.3 = (bf16[256,256]{1,0:T(8,128)(2,1)S(1)}, bf16[256,256]{1,0:T(8,128)(2,1)S(1)}, u32[]{:S(2)}, u32[]{:S(2)}) collective-permute-start(bf16[256,256]{1,0:T(8,128)(2,1)S(1)} %convolution_convert_fusion.2), channel_id=1, source_target_pairs={{0,64},{64,0},{1,65},{65,1},{2,66},{66,2},{3,67},{67,3},{4,68},{68... | collective-permute-start | bytes 393224 | tf_op jit(solution)/shard_map/ppermute | solution.py:79
  158.6 0.7 copy.31
  159.4 0.7 copy.32
  160.1 0.0 all-to-all-done.3
  160.2 8.2 %collective-permute-start.1 = (f32[64,128]{1,0:T(8,128)S(1)}, f32[64,128]{1,0:T(8,128)S(1)}, u32[]{:S(2)}, u32[]{:S(2)}) collective-permute-start(f32[64,128]{1,0:T(8,128)S(1)} %convert_reduce_fusion.1), channel_id=1, source_target_pairs={{0,0},{1,1},{2,2},{3,3},{4,4},{5,5},{6,6},{7,7},{8,128},{9,129},{1... | collective-permute-start | bytes 98312 | tf_op jit(solution)/shard_map/ppermute | solution.py:62
  168.3 0.0 collective-permute-done.3
  168.3 1.0 multiply_convert_fusion
  169.4 8.4 %collective-permute-done.1 = f32[64,128]{1,0:T(8,128)S(1)} collective-permute-done((f32[64,128]{1,0:T(8,128)S(1)}, f32[64,128]{1,0:T(8,128)S(1)}, u32[]{:S(2)}, u32[]{:S(2)}) %collective-permute-start.1) | collective-permute-done | bytes 32800 | tf_op jit(solution)/shard_map/ppermute | solution.py:62
  177.8 0.6 fusion.16
  (6 shorter events, 0.1 us)
Async XLA Ops:
  0.6 41.6 %copy-start = (bf16[256,256]{1,0:T(8,128)(2,1)S(1)}, bf16[256,256]{1,0:T(8,128)(2,1)}, u32[]{:S(2)}) copy-start(bf16[256,256]{1,0:T(8,128)(2,1)} %param.8) | copy-start | bytes 393220
  0.6 12.0 %collective-permute-start.2 = (bf16[64,128]{1,0:T(8,128)(2,1)}, bf16[64,128]{1,0:T(8,128)(2,1)S(1)}, u32[]{:S(2)}, u32[]{:S(2)}) collective-permute-start(bf16[64,128]{1,0:T(8,128)(2,1)} %bitcast.42), channel_id=1, source_target_pairs={{0,0},{1,1},{2,2},{3,3},{4,4},{5,5},{6,6},{7,7},{8,128},{9,129},{1... | collective-permute-start | bytes 49160 | tf_op jit(solution)/shard_map/ppermute | solution.py:41
  30.7 26.1 %all-to-all-start.5 = ((bf16[4,8,64,128]{3,2,1,0:T(8,128)(2,1)}), bf16[4,8,64,128]{3,2,1,0:T(8,128)(2,1)S(1)}, u32[]{:S(2)}, u32[]{:S(2)}) async-start(bf16[4,8,64,128]{3,2,1,0:T(8,128)(2,1)} %broadcast_in_dim.10), calls=%async_computation.5 | async-start | bytes 1048576 | tf_op jit(solution)/shard_map/all_to_all | solution.py:29
  42.3 14.5 %collective-permute-start = (bf16[256,256]{1,0:T(8,128)(2,1)S(1)}, bf16[256,256]{1,0:T(8,128)(2,1)S(1)}, u32[]{:S(2)}, u32[]{:S(2)}) collective-permute-start(bf16[256,256]{1,0:T(8,128)(2,1)S(1)} %copy-done), channel_id=1, source_target_pairs={{0,64},{64,0},{1,65},{65,1},{2,66},{66,2},{3,67},{67,3},{4,68},{68... | collective-permute-start | bytes 393224 | tf_op jit(solution)/shard_map/ppermute | solution.py:40
  73.5 10.9 %copy-start.1 = (bf16[128,256]{1,0:T(8,128)(2,1)S(1)}, bf16[128,256]{1,0:T(8,128)(2,1)}, u32[]{:S(2)}) copy-start(bf16[128,256]{1,0:T(8,128)(2,1)} %param.5) | copy-start | bytes 196612
  73.5 11.0 %copy-start.2 = (bf16[128,256]{1,0:T(8,128)(2,1)S(1)}, bf16[128,256]{1,0:T(8,128)(2,1)}, u32[]{:S(2)}) copy-start(bf16[128,256]{1,0:T(8,128)(2,1)} %param.6) | copy-start | bytes 196612
  74.4 25.5 %all-to-all-start.7 = ((bf16[8,128,256]{1,2,0:T(8,128)(2,1)}), bf16[8,128,256]{1,2,0:T(8,128)(2,1)S(1)}, u32[]{:S(2)}, u32[]{:S(2)}) async-start(bf16[8,128,256]{1,2,0:T(8,128)(2,1)} %bitcast.36), calls=%async_computation.7 | async-start | bytes 1048576 | tf_op jit(solution)/shard_map/all_to_all | solution.py:33
  101.0 21.7 %all-to-all-start = ((bf16[8,128,256]{2,1,0:T(8,128)(2,1)}), bf16[8,128,256]{2,1,0:T(8,128)(2,1)S(1)}, u32[]{:S(2)}, u32[]{:S(2)}) async-start(bf16[8,128,256]{2,1,0:T(8,128)(2,1)} %broadcast_in_dim.8), calls=%async_computation | async-start | bytes 1048576 | tf_op jit(solution)/shard_map/all_to_all | solution.py:29
  142.8 17.4 %all-to-all-start.3 = ((bf16[8,64,128]{2,1,0:T(8,128)(2,1)}), bf16[8,64,128]{2,1,0:T(8,128)(2,1)S(1)}, u32[]{:S(2)}, u32[]{:S(2)}) async-start(bf16[8,64,128]{2,1,0:T(8,128)(2,1)} %bitcast.8), calls=%async_computation.3 | async-start | bytes 262144 | tf_op jit(solution)/shard_map/all_to_all | solution.py:33
  146.9 30.9 %copy-start.3 = (bf16[128,64]{0,1:T(8,128)(2,1)S(1)}, bf16[128,64]{0,1:T(8,128)(2,1)}, u32[]{:S(2)}) copy-start(bf16[128,64]{0,1:T(8,128)(2,1)} %param.7) | copy-start | bytes 49156
  146.9 21.4 %collective-permute-start.3 = (bf16[256,256]{1,0:T(8,128)(2,1)S(1)}, bf16[256,256]{1,0:T(8,128)(2,1)S(1)}, u32[]{:S(2)}, u32[]{:S(2)}) collective-permute-start(bf16[256,256]{1,0:T(8,128)(2,1)S(1)} %convolution_convert_fusion.2), channel_id=1, source_target_pairs={{0,64},{64,0},{1,65},{65,1},{2,66},{66,2},{3,67},{67,3},{4,68},{68... | collective-permute-start | bytes 393224 | tf_op jit(solution)/shard_map/ppermute | solution.py:79
  160.2 17.6 %collective-permute-start.1 = (f32[64,128]{1,0:T(8,128)S(1)}, f32[64,128]{1,0:T(8,128)S(1)}, u32[]{:S(2)}, u32[]{:S(2)}) collective-permute-start(f32[64,128]{1,0:T(8,128)S(1)} %convert_reduce_fusion.1), channel_id=1, source_target_pairs={{0,0},{1,1},{2,2},{3,3},{4,4},{5,5},{6,6},{7,7},{8,128},{9,129},{1... | collective-permute-start | bytes 98312 | tf_op jit(solution)/shard_map/ppermute | solution.py:62

commit v2 on v1

v2 whole, which is shorter than its diff:
```python
import math

import jax
import jax.numpy as jnp
from jax import lax
from jax.experimental import pallas as pl
from jax.experimental.pallas import tpu as pltpu
from jax.sharding import Mesh
from jax.sharding import PartitionSpec as P

AXES = ("y", "zh", "x", "zl", "c")
SIZES = (8, 2, 4, 8, 2)
BF, F32 = jnp.bfloat16, jnp.float32
ACROSS = [(0, 1), (1, 0)]


def swap_pairs():
    def at(y, zh, x, zl, c):
        return (((y * 2 + zh) * 4 + x) * 8 + zl) * 2 + c

    return [
        (at(y, zh, x, zl, c), at(2 * x + zl // 4, zh, y // 2, 4 * (y % 2) + zl % 4, c))
        for y in range(8)
        for zh in range(2)
        for x in range(4)
        for zl in range(8)
        for c in range(2)
    ]


def in_vmem(kernel, out_shapes, flops, *operands, scratch=()):
    spec = pl.BlockSpec(memory_space=pltpu.VMEM)
    moved = sum(math.prod(a.shape) * a.dtype.itemsize for a in (*operands, *out_shapes))
    return pl.pallas_call(
        kernel,
        out_shape=out_shapes,
        in_specs=[spec] * len(operands),
        out_specs=[spec] * len(out_shapes),
        scratch_shapes=list(scratch),
        compiler_params=pltpu.CompilerParams(vmem_limit_bytes=32 * 1024 * 1024),
        cost_estimate=pl.CostEstimate(flops=flops, bytes_accessed=moved, transcendentals=0),
    )(*operands)


def shape(dims, dtype=BF):
    return jax.ShapeDtypeStruct(dims, dtype)


def hidden_kernel(gate_ref, up_ref, out_ref):
    gate = gate_ref[...].astype(F32)
    hidden = (gate * jax.nn.sigmoid(gate) * up_ref[...].astype(F32)).astype(BF)
    for i in range(8):
        out_ref[i] = hidden


def proj_kernel(hid_ref, own_ref, other_ref, keep_ref, send_ref):
    zh, core = lax.axis_index("zh"), lax.axis_index("c")
    hid = hid_ref[...].reshape(1024, 256)
    for l in range(4):
        cols = slice((l % 2) * 128, (l % 2) * 128 + 128)
        w = jnp.where(zh == l // 2, own_ref[:, cols], other_ref[:, cols])
        res = lax.dot_general(w, hid, (((0,), (1,)), ((), ())), preferred_element_type=F32).astype(BF)
        first, second = res[:64], res[64:]
        keep = jnp.where(core == 0, first, second)
        send = jnp.where(core == 0, second, first)
        for g in range(8):
            toks = slice(g * 128, g * 128 + 128)
            keep_ref[g // 2, (g % 2) * 4 + l] = keep[:, toks]
            send_ref[g // 2, (g % 2) * 4 + l] = send[:, toks]


def grad_kernel(hid_ref, cot_ref, own_ref, other_ref, partial_ref, keep_ref, send_ref, rows_ref):
    zh = lax.axis_index("zh")
    for g in range(8):
        for l in range(4):
            for c in range(2):
                rows_ref[(2 * l + c) * 64 : (2 * l + c) * 64 + 64, g * 128 : g * 128 + 128] = cot_ref[
                    g // 2, c, (g % 2) * 4 + l
                ]
    own, other = own_ref[...], other_ref[...]
    low = jnp.where(zh == 0, own, other)
    high = jnp.where(zh == 0, other, own)
    weights = jnp.concatenate([low, high], axis=1)
    for g in range(8):
        partial_ref[g] = lax.dot_general(
            rows_ref[:, g * 128 : g * 128 + 128],
            weights,
            (((0,), (1,)), ((), ())),
            preferred_element_type=F32,
        ).astype(BF)
    hid = hid_ref[...].reshape(1024, 256)
    first = lax.dot_general(hid, rows_ref[:256], (((0,), (1,)), ((), ())), preferred_element_type=F32)
    second = lax.dot_general(hid, rows_ref[256:], (((0,), (1,)), ((), ())), preferred_element_type=F32)
    keep_ref[...] = jnp.where(zh == 0, first, second)
    send_ref[...] = jnp.where(zh == 0, second, first).astype(BF)


def after(value, *deps):
    return lax.optimization_barrier((value, *deps))[0]


def gather(part, axis):
    return lax.all_to_all(jnp.broadcast_to(part[None], (lax.axis_size(axis),) + part.shape), axis, 0, 0)


def scatter_sum(parts, axis):
    return jnp.sum(lax.all_to_all(parts, axis, 0, 0).astype(F32), axis=0)


def body(gate_input, up_input, residual, down_proj, cotangent):
    swap = swap_pairs()
    cot_moved = lax.ppermute(cotangent.T, AXES, swap)
    w_other = lax.ppermute(down_proj, "zh", ACROSS)

    (spread,) = in_vmem(hidden_kernel, [shape((8, 128, 256))], 500_000, gate_input, up_input)
    hid = lax.all_to_all(spread, "y", 0, 0)

    cot_line = gather(after(cot_moved, hid), "zl")
    cot = lax.all_gather(cot_line, ("x", "c"), axis=0, tiled=False)
    cot = cot.reshape(4, 2, 8, 64, 128)

    hid_now, w_now = lax.optimization_barrier((hid, w_other, cot_line))[:2]
    keep, send = in_vmem(
        proj_kernel, [shape((4, 8, 64, 128))] * 2, 2 * 1024 * 256 * 512, hid_now, down_proj, w_now
    )
    proj = (keep.astype(F32) + lax.ppermute(send, "c", ACROSS).astype(F32)).astype(BF)
    proj = scatter_sum(proj, "x").astype(BF)
    proj = scatter_sum(proj, "zl")

    cot_now = after(cot, proj)
    partial, term, term_out = in_vmem(
        grad_kernel,
        [shape((8, 128, 256)), shape((256, 256), F32), shape((256, 256))],
        4 * 1024 * 256 * 512,
        hid,
        cot_now,
        down_proj,
        w_now,
        scratch=[pltpu.VMEM((512, 1024), BF)],
    )
    moved = lax.ppermute(proj, AXES, swap)
    term_in = lax.ppermute(term_out, "zh", ACROSS)
    hidden_grad = scatter_sum(partial, "y")

    gate = gate_input.astype(F32)
    up = up_input.astype(F32)
    sig = jax.nn.sigmoid(gate)
    up_grad = (hidden_grad * gate * sig).astype(BF)
    gate_grad = (hidden_grad * up * sig * (1.0 + gate * (1.0 - sig))).astype(BF)
    layer_out = (residual.astype(F32).T + moved).astype(BF).T
    down_grad = ((term + term_in.astype(F32)) * (1.0 / math.sqrt(2048))).astype(BF)
    return (layer_out, gate_grad, up_grad, down_grad)


def solution(mesh):
    fine = Mesh(mesh.devices.reshape(SIZES), AXES)
    dp, tensor = ("y", "zh"), ("x", "zl", "c")
    in_specs = (P(dp, tensor), P(dp, tensor), P(dp, tensor), P(tensor, dp), P(dp, tensor))
    out_specs = (P(dp, tensor), P(dp, tensor), P(dp, tensor), P(tensor, dp))
    return jax.shard_map(body, mesh=fine, in_specs=in_specs, out_specs=out_specs, check_vma=False)
```

time: 179 us -> 162 us (0.905)
  the two profiles are of different devices: /device:TPU:9 before, /device:TPU:12 now
where the time goes in v2:
time: 162 us
  starting transfers between devices  78.5 us (48%)
  blocking collectives  41.6 us (26%)
  waiting for transfers between devices  16.5 us (10%)
  between operations  14.2 us (9%)
  local copies, waits for them, and re-layouts  5.02 us (3%)
  Pallas kernels  3.42 us (2%)
  other arithmetic  2.37 us (1%)
    all_to_all x2, blocking collectives, scatter_sum(): return jnp.sum(lax.all_to_all(parts, axis, 0, 0).astype(F32), axis=0)  41.6 us
    all_to_all x1, starting transfers between devices, gather(): lax.all_to_all(jnp.broadcast_to(part[None], (lax.axis_size(axis),) + part...  15.8 us
    ppermute x1, starting transfers between devices, body(): cot_moved = lax.ppermute(cotangent.T, AXES, swap)  14.8 us
    ppermute x1, starting transfers between devices, body(): w_other = lax.ppermute(down_proj, 'zh', ACROSS)  11.9 us
    ppermute x1, starting transfers between devices, body(): term_in = lax.ppermute(term_out, 'zh', ACROSS)  10.5 us
    ppermute x1, waiting for transfers between devices, body(): term_in = lax.ppermute(term_out, 'zh', ACROSS)  9.51 us
    ppermute x1, starting transfers between devices, body(): moved = lax.ppermute(proj, AXES, swap)  8.38 us
    all_to_all x1, starting transfers between devices, body(): hid = lax.all_to_all(spread, 'y', 0, 0)  7.68 us
  transfers between devices with their start and end apart: 9, of which 4 were waited for; matrix products, arithmetic and copies ran while one was open for 1% of the time, Pallas kernels for 1%

profile of v2, /device:TPU:12, one launch (start us, length us, event | category | flops | bytes accessed | tf_op | source)
XLA Modules:
  0.0 161.6 jit_solution(12911348165761435687)
XLA Ops:
  7.2 0.0 copy-start
  7.2 0.8 copy-done
  8.0 0.0 copy-start.2
  8.0 0.8 copy-done.2
  8.8 0.8 shard_map.84
  9.7 0.0 copy-start.8
  9.7 7.7 %all-to-all-start = ((bf16[8,128,256]{2,1,0:T(8,128)(2,1)}), bf16[8,128,256]{2,1,0:T(8,128)(2,1)S(1)}, u32[]{:S(2)}, u32[]{:S(2)}) async-start(bf16[8,128,256]{2,1,0:T(8,128)(2,1)} %shard_map.84), calls=%async_computation | async-start | bytes 1048576 | tf_op jit(solution)/shard_map/all_to_all | solution.py:116
  17.4 0.0 copy-done.8
  17.4 14.8 %collective-permute-start.1 = (bf16[64,128]{1,0:T(8,128)(2,1)S(1)}, bf16[64,128]{1,0:T(8,128)(2,1)S(1)}, u32[]{:S(2)}, u32[]{:S(2)}) collective-permute-start(bf16[64,128]{1,0:T(8,128)(2,1)S(1)} %bitcast.11), channel_id=1, source_target_pairs={{0,0},{1,1},{2,2},{3,3},{4,4},{5,5},{6,6},{7,7},{8,128},{9,129},{1... | collective-permute-start | bytes 49160 | tf_op jit(solution)/shard_map/ppermute | solution.py:112
  32.1 1.9 %collective-permute-done.1 = bf16[64,128]{1,0:T(8,128)(2,1)S(1)} collective-permute-done((bf16[64,128]{1,0:T(8,128)(2,1)S(1)}, bf16[64,128]{1,0:T(8,128)(2,1)S(1)}, u32[]{:S(2)}, u32[]{:S(2)}) %collective-permute-start.1) | collective-permute-done | bytes 16416 | tf_op jit(solution)/shard_map/ppermute | solution.py:112
  34.0 0.0 all-to-all-done.hid_ref
  34.0 0.7 broadcast_in_dim.2
  34.7 0.0 copy-start.5
  34.7 15.8 %all-to-all-start.1 = ((bf16[8,64,128]{2,1,0:T(8,128)(2,1)}), bf16[8,64,128]{2,1,0:T(8,128)(2,1)S(1)}, u32[]{:S(2)}, u32[]{:S(2)}) async-start(bf16[8,64,128]{2,1,0:T(8,128)(2,1)} %broadcast_in_dim.2), calls=%async_computation.1 | async-start | bytes 262144 | tf_op jit(solution)/shard_map/all_to_all | solution.py:103
  50.4 0.0 all-gather.3.cloned.1.call-start
  50.5 0.0 copy-done.5
  50.5 11.9 %collective-permute-start = (bf16[256,256]{1,0:T(8,128)(2,1)S(1)}, bf16[256,256]{1,0:T(8,128)(2,1)S(1)}, u32[]{:S(2)}, u32[]{:S(2)}) collective-permute-start(bf16[256,256]{1,0:T(8,128)(2,1)S(1)} %copy-done.5), channel_id=1, source_target_pairs={{0,64},{64,0},{1,65},{65,1},{2,66},{66,2},{3,67},{67,3},{4,68},{68... | collective-permute-start | bytes 393224 | tf_op jit(solution)/shard_map/ppermute | solution.py:113
  62.4 0.0 all-to-all-done.1
  62.4 0.0 copy-start.6
  62.4 0.6 copy-done.6
  63.0 0.0 all-gather.3.cloned.1.call-update
  63.1 3.2 %collective-permute-done.other_ref = bf16[256,256]{1,0:T(8,128)(2,1)S(1)} collective-permute-done((bf16[256,256]{1,0:T(8,128)(2,1)S(1)}, bf16[256,256]{1,0:T(8,128)(2,1)S(1)}, u32[]{:S(2)}, u32[]{:S(2)}) %collective-permute-start) | collective-permute-done | bytes 131104 | tf_op jit(solution)/shard_map/ppermute | solution.py:113
  66.2 0.8 shard_map.85
  67.1 1.9 %collective-permute-start.2 = (bf16[4,8,64,128]{3,2,1,0:T(8,128)(2,1)S(1)}, bf16[4,8,64,128]{3,2,1,0:T(8,128)(2,1)S(1)}, u32[]{:S(2)}, u32[]{:S(2)}) collective-permute-start(bf16[4,8,64,128]{3,2,1,0:T(8,128)(2,1)S(1)} %get-tuple-element.17), channel_id=1, source_target_pairs={{0,1},{1,0},{2,3},{3,2},{4,5},{5,4},{6,7},{7,6},{8,9},{9,8},{10,11... | collective-permute-start | bytes 1572872 | tf_op jit(solution)/shard_map/ppermute | solution.py:126
  69.0 1.9 %collective-permute-done.2 = bf16[4,8,64,128]{3,2,1,0:T(8,128)(2,1)S(1)} collective-permute-done((bf16[4,8,64,128]{3,2,1,0:T(8,128)(2,1)S(1)}, bf16[4,8,64,128]{3,2,1,0:T(8,128)(2,1)S(1)}, u32[]{:S(2)}, u32[]{:S(2)}) %collective-permute-start.2) | collective-permute-done | bytes 524320 | tf_op jit(solution)/shard_map/ppermute | solution.py:126
  70.9 0.2 add_convert_fusion
  71.1 11.7 %all_to_all.25 = bf16[4,8,64,128]{3,2,1,0:T(8,128)(2,1)S(1)} all-to-all(bf16[4,8,64,128]{3,2,1,0:T(8,128)(2,1)S(1)} %add_convert_fusion), channel_id=1, replica_groups=mesh['y'=8,'zh'=2,'x'=4,'zl'=8,'c'=2] {'x'}, dimensions={0} | all-to-all | bytes 1048576 | tf_op jit(solution)/shard_map/all_to_all | solution.py:107
  82.7 0.1 reduce_sum.30
  82.8 29.9 %all_to_all.26 = bf16[8,64,128]{2,1,0:T(8,128)(2,1)S(1)} all-to-all(bf16[8,64,128]{2,1,0:T(8,128)(2,1)S(1)} %reduce_sum.30), channel_id=1, replica_groups=mesh['y'=8,'zh'=2,'x'=4,'zl'=8,'c'=2] {'zl'}, dimensions={0} | all-to-all | bytes 262144 | tf_op jit(solution)/shard_map/all_to_all | solution.py:107
  112.8 0.0 all-gather.3.cloned.1.call-done
  112.8 0.0 copy-start.4
  112.8 1.2 copy-done.4
  114.0 1.8 %shard_map.86 = (bf16[8,128,256]{2,1,0:T(8,128)(2,1)}, f32[256,256]{1,0:T(8,128)S(1)}, bf16[256,256]{1,0:T(8,128)(2,1)S(1)}) custom-call(bf16[8,128,256]{2,1,0:T(8,128)(2,1)S(1)} %all-to-all-done.hid_ref, bf16[4,2,8,64,128]{4,3,2,1,0:T(8,128)(2,1)S(1)} %bitcast.10, bf16[256,256]{1,0:T(8,128)(2,1)S(1)} %copy-done.5, ...), custom_call_target="tpu_custom_call" | custom-call | flops 536870912 | bytes 2752512 | tf_op jit(solution)/shard_map/pallas_call | solution.py:34
  115.8 0.0 copy-start.7
  115.8 7.6 %all-to-all-start.4 = ((bf16[8,128,256]{2,1,0:T(8,128)(2,1)}), bf16[8,128,256]{2,1,0:T(8,128)(2,1)S(1)}, u32[]{:S(2)}, u32[]{:S(2)}) async-start(bf16[8,128,256]{2,1,0:T(8,128)(2,1)} %get-tuple-element.19), calls=%async_computation.4 | async-start | bytes 1048576 | tf_op jit(solution)/shard_map/all_to_all | solution.py:107
  123.4 8.4 %collective-permute-start.3 = (f32[64,128]{1,0:T(8,128)S(1)}, f32[64,128]{1,0:T(8,128)S(1)}, u32[]{:S(2)}, u32[]{:S(2)}) collective-permute-start(f32[64,128]{1,0:T(8,128)S(1)} %convert_reduce_fusion.1), channel_id=1, source_target_pairs={{0,0},{1,1},{2,2},{3,3},{4,4},{5,5},{6,6},{7,7},{8,128},{9,129},{1... | collective-permute-start | bytes 98312 | tf_op jit(solution)/shard_map/ppermute | solution.py:141
  131.8 10.5 %collective-permute-start.4 = (bf16[256,256]{1,0:T(8,128)(2,1)S(1)}, bf16[256,256]{1,0:T(8,128)(2,1)S(1)}, u32[]{:S(2)}, u32[]{:S(2)}) collective-permute-start(bf16[256,256]{1,0:T(8,128)(2,1)S(1)} %get-tuple-element.21), channel_id=1, source_target_pairs={{0,64},{64,0},{1,65},{65,1},{2,66},{66,2},{3,67},{67,3},{4,68},{68... | collective-permute-start | bytes 393224 | tf_op jit(solution)/shard_map/ppermute | solution.py:142
  142.3 0.0 collective-permute-done.3
  142.4 0.0 copy-done.7
  142.4 0.6 fusion.9
  143.0 9.5 %collective-permute-done.4 = bf16[256,256]{1,0:T(8,128)(2,1)S(1)} collective-permute-done((bf16[256,256]{1,0:T(8,128)(2,1)S(1)}, bf16[256,256]{1,0:T(8,128)(2,1)S(1)}, u32[]{:S(2)}, u32[]{:S(2)}) %collective-permute-start.4) | collective-permute-done | bytes 131104 | tf_op jit(solution)/shard_map/ppermute | solution.py:142
  152.5 0.7 multiply_convert_fusion
  153.2 0.0 copy-start.3
  153.2 0.0 all-to-all-done.4
  153.2 0.1 convert_reduce_fusion
  153.3 0.8 copy-done.1
  154.0 0.0 copy-done.3
  154.0 0.7 fusion.7
  (2 shorter events, 0.0 us)
Async XLA Ops:
  7.2 0.8 copy-start
  8.0 0.8 copy-start.2
  9.7 7.7 %copy-start.8 = (bf16[128,64]{0,1:T(8,128)(2,1)S(1)}, bf16[128,64]{0,1:T(8,128)(2,1)}, u32[]{:S(2)}) copy-start(bf16[128,64]{0,1:T(8,128)(2,1)} %param.9) | copy-start | bytes 49156
  9.7 24.3 %all-to-all-start = ((bf16[8,128,256]{2,1,0:T(8,128)(2,1)}), bf16[8,128,256]{2,1,0:T(8,128)(2,1)S(1)}, u32[]{:S(2)}, u32[]{:S(2)}) async-start(bf16[8,128,256]{2,1,0:T(8,128)(2,1)} %shard_map.84), calls=%async_computation | async-start | bytes 1048576 | tf_op jit(solution)/shard_map/all_to_all | solution.py:116
  17.4 16.6 %collective-permute-start.1 = (bf16[64,128]{1,0:T(8,128)(2,1)S(1)}, bf16[64,128]{1,0:T(8,128)(2,1)S(1)}, u32[]{:S(2)}, u32[]{:S(2)}) collective-permute-start(bf16[64,128]{1,0:T(8,128)(2,1)S(1)} %bitcast.11), channel_id=1, source_target_pairs={{0,0},{1,1},{2,2},{3,3},{4,4},{5,5},{6,6},{7,7},{8,128},{9,129},{1... | collective-permute-start | bytes 49160 | tf_op jit(solution)/shard_map/ppermute | solution.py:112
  34.7 15.8 %copy-start.5 = (bf16[256,256]{1,0:T(8,128)(2,1)S(1)}, bf16[256,256]{1,0:T(8,128)(2,1)}, u32[]{:S(2)}) copy-start(bf16[256,256]{1,0:T(8,128)(2,1)} %own_ref.3) | copy-start | bytes 393220
  34.7 27.7 %all-to-all-start.1 = ((bf16[8,64,128]{2,1,0:T(8,128)(2,1)}), bf16[8,64,128]{2,1,0:T(8,128)(2,1)S(1)}, u32[]{:S(2)}, u32[]{:S(2)}) async-start(bf16[8,64,128]{2,1,0:T(8,128)(2,1)} %broadcast_in_dim.2), calls=%async_computation.1 | async-start | bytes 262144 | tf_op jit(solution)/shard_map/all_to_all | solution.py:103
  50.4 62.4 %all-gather.3.cloned.1.call-start = ((), (), s32[]{:S(2)}) async-start(), calls=%async_computation.5 | async-start | bytes 1179648 | tf_op jit(solution)/shard_map/all_gather | solution.py:119
  50.5 15.7 %collective-permute-start = (bf16[256,256]{1,0:T(8,128)(2,1)S(1)}, bf16[256,256]{1,0:T(8,128)(2,1)S(1)}, u32[]{:S(2)}, u32[]{:S(2)}) collective-permute-start(bf16[256,256]{1,0:T(8,128)(2,1)S(1)} %copy-done.5), channel_id=1, source_target_pairs={{0,64},{64,0},{1,65},{65,1},{2,66},{66,2},{3,67},{67,3},{4,68},{68... | collective-permute-start | bytes 393224 | tf_op jit(solution)/shard_map/ppermute | solution.py:113
  62.4 0.7 copy-start.6
  67.1 3.8 %collective-permute-start.2 = (bf16[4,8,64,128]{3,2,1,0:T(8,128)(2,1)S(1)}, bf16[4,8,64,128]{3,2,1,0:T(8,128)(2,1)S(1)}, u32[]{:S(2)}, u32[]{:S(2)}) collective-permute-start(bf16[4,8,64,128]{3,2,1,0:T(8,128)(2,1)S(1)} %get-tuple-element.17), channel_id=1, source_target_pairs={{0,1},{1,0},{2,3},{3,2},{4,5},{5,4},{6,7},{7,6},{8,9},{9,8},{10,11... | collective-permute-start | bytes 1572872 | tf_op jit(solution)/shard_map/ppermute | solution.py:126
  112.8 1.2 copy-start.4
  115.8 26.6 %copy-start.7 = (bf16[128,64]{0,1:T(8,128)(2,1)S(1)}, bf16[128,64]{0,1:T(8,128)(2,1)}, u32[]{:S(2)}) copy-start(bf16[128,64]{0,1:T(8,128)(2,1)} %param.7) | copy-start | bytes 49156
  115.8 37.4 %all-to-all-start.4 = ((bf16[8,128,256]{2,1,0:T(8,128)(2,1)}), bf16[8,128,256]{2,1,0:T(8,128)(2,1)S(1)}, u32[]{:S(2)}, u32[]{:S(2)}) async-start(bf16[8,128,256]{2,1,0:T(8,128)(2,1)} %get-tuple-element.19), calls=%async_computation.4 | async-start | bytes 1048576 | tf_op jit(solution)/shard_map/all_to_all | solution.py:107
  123.4 18.9 %collective-permute-start.3 = (f32[64,128]{1,0:T(8,128)S(1)}, f32[64,128]{1,0:T(8,128)S(1)}, u32[]{:S(2)}, u32[]{:S(2)}) collective-permute-start(f32[64,128]{1,0:T(8,128)S(1)} %convert_reduce_fusion.1), channel_id=1, source_target_pairs={{0,0},{1,1},{2,2},{3,3},{4,4},{5,5},{6,6},{7,7},{8,128},{9,129},{1... | collective-permute-start | bytes 98312 | tf_op jit(solution)/shard_map/ppermute | solution.py:141
  131.8 20.7 %collective-permute-start.4 = (bf16[256,256]{1,0:T(8,128)(2,1)S(1)}, bf16[256,256]{1,0:T(8,128)(2,1)S(1)}, u32[]{:S(2)}, u32[]{:S(2)}) collective-permute-start(bf16[256,256]{1,0:T(8,128)(2,1)S(1)} %get-tuple-element.21), channel_id=1, source_target_pairs={{0,64},{64,0},{1,65},{65,1},{2,66},{66,2},{3,67},{67,3},{4,68},{68... | collective-permute-start | bytes 393224 | tf_op jit(solution)/shard_map/ppermute | solution.py:142
  153.2 0.8 copy-start.1
  153.2 0.9 copy-start.3
Sparse Core Ops, SparseCore 0:
  63.2 37.3 all-gather.2

commit v3 on v2

--- a/solution.py
+++ b/solution.py
@@ -69,14 +69,27 @@
             send_ref[g // 2, (g % 2) * 4 + l] = send[:, toks]
 
 
-def grad_kernel(hid_ref, cot_ref, own_ref, other_ref, partial_ref, keep_ref, send_ref, rows_ref):
-    zh = lax.axis_index("zh")
-    for g in range(8):
-        for l in range(4):
-            for c in range(2):
-                rows_ref[(2 * l + c) * 64 : (2 * l + c) * 64 + 64, g * 128 : g * 128 + 128] = cot_ref[
-                    g // 2, c, (g % 2) * 4 + l
-                ]
+def pack_kernel(cot_ref, keep_ref, came_ref, out_ref):
+    total = (keep_ref[...].astype(F32) + came_ref[...].astype(F32)).astype(BF)
+    for x in range(4):
+        out_ref[x, :8] = cot_ref[...]
+        out_ref[x, 8:] = total[x]
+
+
+def unpack_kernel(got_ref, cot_ref, sum_ref):
+    cot_ref[...] = got_ref[:, :8]
+    sum_ref[...] = jnp.sum(got_ref[:, 8:].astype(F32), axis=0).astype(BF)
+
+
+def grad_kernel(hid_ref, mine_ref, its_ref, own_ref, other_ref, partial_ref, keep_ref, send_ref, rows_ref):
+    zh, core = lax.axis_index("zh"), lax.axis_index("c")
+    for l in range(4):
+        here = pl.ds(pl.multiple_of((2 * l + core) * 64, 64), 64)
+        there = pl.ds(pl.multiple_of((2 * l + 1 - core) * 64, 64), 64)
+        for g in range(8):
+            toks = slice(g * 128, g * 128 + 128)
+            rows_ref[here, toks] = mine_ref[g // 2, (g % 2) * 4 + l]
+            rows_ref[there, toks] = its_ref[g // 2, (g % 2) * 4 + l]
     own, other = own_ref[...], other_ref[...]
     low = jnp.where(zh == 0, own, other)
     high = jnp.where(zh == 0, other, own)
@@ -115,25 +128,34 @@
     (spread,) = in_vmem(hidden_kernel, [shape((8, 128, 256))], 500_000, gate_input, up_input)
     hid = lax.all_to_all(spread, "y", 0, 0)
 
-    cot_line = gather(after(cot_moved, hid), "zl")
-    cot = lax.all_gather(cot_line, ("x", "c"), axis=0, tiled=False)
-    cot = cot.reshape(4, 2, 8, 64, 128)
+    cot_moved, w_now = lax.optimization_barrier((cot_moved, w_other, hid))[:2]
+    cot_line = gather(cot_moved, "zl")
 
-    hid_now, w_now = lax.optimization_barrier((hid, w_other, cot_line))[:2]
     keep, send = in_vmem(
-        proj_kernel, [shape((4, 8, 64, 128))] * 2, 2 * 1024 * 256 * 512, hid_now, down_proj, w_now
+        proj_kernel,
+        [shape((4, 8, 64, 128))] * 2,
+        2 * 1024 * 256 * 512,
+        after(hid, cot_line),
+        down_proj,
+        w_now,
     )
-    proj = (keep.astype(F32) + lax.ppermute(send, "c", ACROSS).astype(F32)).astype(BF)
-    proj = scatter_sum(proj, "x").astype(BF)
+    came = lax.ppermute(send, "c", ACROSS)
+    (packed,) = in_vmem(pack_kernel, [shape((4, 16, 64, 128))], 300_000, cot_line, keep, came)
+    mine, proj = in_vmem(
+        unpack_kernel,
+        [shape((4, 8, 64, 128)), shape((8, 64, 128))],
+        300_000,
+        lax.all_to_all(packed, "x", 0, 0),
+    )
+    its = lax.ppermute(mine, "c", ACROSS)
     proj = scatter_sum(proj, "zl")
-
-    cot_now = after(cot, proj)
     partial, term, term_out = in_vmem(
         grad_kernel,
         [shape((8, 128, 256)), shape((256, 256), F32), shape((256, 256))],
         4 * 1024 * 256 * 512,
         hid,
-        cot_now,
+        mine,
+        after(its, proj),
         down_proj,
         w_now,
         scratch=[pltpu.VMEM((512, 1024), BF)],

time: 162 us -> 145 us (0.90)
  the two profiles are of different devices: /device:TPU:12 before, /device:TPU:4 now
where the time goes in v3:
time: 145 us
  starting transfers between devices  65.1 us (45%)
  blocking collectives  42.7 us (29%)
  waiting for transfers between devices  26.9 us (19%)
  Pallas kernels  4.41 us (3%)
  local copies, waits for them, and re-layouts  2.5 us (2%)
  other arithmetic  2.11 us (1%)
    all_to_all x1, blocking collectives, gather(): lax.all_to_all(jnp.broadcast_to(part[None], (lax.axis_size(axis),) + part...  25.4 us
    ppermute x1, starting transfers between devices, body(): w_other = lax.ppermute(down_proj, 'zh', ACROSS)  19.4 us
    all_to_all x1, blocking collectives, body(): lax.all_to_all(packed, 'x', 0, 0)  17.3 us
    ppermute x1, waiting for transfers between devices, body(): term_in = lax.ppermute(term_out, 'zh', ACROSS)  11.3 us
    ppermute x1, starting transfers between devices, body(): moved = lax.ppermute(proj, AXES, swap)  9.89 us
    all_to_all x2, waiting for transfers between devices, scatter_sum(): return jnp.sum(lax.all_to_all(parts, axis, 0, 0).astype(F32), axis=0)  9.54 us
    ppermute x1, starting transfers between devices, body(): term_in = lax.ppermute(term_out, 'zh', ACROSS)  9.13 us
    all_to_all x2, starting transfers between devices, scatter_sum(): return jnp.sum(lax.all_to_all(parts, axis, 0, 0).astype(F32), axis=0)  7.92 us
  transfers between devices with their start and end apart: 9, of which 4 were waited for; matrix products, arithmetic and copies ran while one was open for 1% of the time, Pallas kernels for 0%

profile of v3, /device:TPU:4, one launch (start us, length us, event | category | flops | bytes accessed | tf_op | source)
XLA Modules:
  0.0 144.5 jit_solution(215157537711383998)
XLA Ops:
  0.6 0.0 copy-start
  0.6 0.8 copy-done
  1.5 0.0 copy-start.2
  1.5 0.8 copy-done.2
  2.3 0.8 shard_map.84
  3.1 0.0 copy-start.4
  3.1 0.0 copy-start.6
  3.2 7.2 %all-to-all-start = ((bf16[8,128,256]{2,1,0:T(8,128)(2,1)}), bf16[8,128,256]{2,1,0:T(8,128)(2,1)S(1)}, u32[]{:S(2)}, u32[]{:S(2)}) async-start(bf16[8,128,256]{2,1,0:T(8,128)(2,1)} %shard_map.84), calls=%async_computation | async-start | bytes 1048576 | tf_op jit(solution)/shard_map/all_to_all | solution.py:129
  10.4 0.0 copy-done.4
  10.4 19.4 %collective-permute-start.1 = (bf16[256,256]{1,0:T(8,128)(2,1)S(1)}, bf16[256,256]{1,0:T(8,128)(2,1)S(1)}, u32[]{:S(2)}, u32[]{:S(2)}) collective-permute-start(bf16[256,256]{1,0:T(8,128)(2,1)S(1)} %copy-done.4), channel_id=1, source_target_pairs={{0,64},{64,0},{1,65},{65,1},{2,66},{66,2},{3,67},{67,3},{4,68},{68... | collective-permute-start | bytes 393224 | tf_op jit(solution)/shard_map/ppermute | solution.py:126
  29.8 0.0 copy-done.6
  29.8 7.8 %collective-permute-start = (bf16[64,128]{1,0:T(8,128)(2,1)S(1)}, bf16[64,128]{1,0:T(8,128)(2,1)S(1)}, u32[]{:S(2)}, u32[]{:S(2)}) collective-permute-start(bf16[64,128]{1,0:T(8,128)(2,1)S(1)} %bitcast.9), channel_id=1, source_target_pairs={{0,0},{1,1},{2,2},{3,3},{4,4},{5,5},{6,6},{7,7},{8,128},{9,129},{1... | collective-permute-start | bytes 49160 | tf_op jit(solution)/shard_map/ppermute | solution.py:125
  37.5 4.2 %collective-permute-done = bf16[64,128]{1,0:T(8,128)(2,1)S(1)} collective-permute-done((bf16[64,128]{1,0:T(8,128)(2,1)S(1)}, bf16[64,128]{1,0:T(8,128)(2,1)S(1)}, u32[]{:S(2)}, u32[]{:S(2)}) %collective-permute-start) | collective-permute-done | bytes 16416 | tf_op jit(solution)/shard_map/ppermute | solution.py:125
  41.7 0.0 collective-permute-done.1.other_ref
  41.7 0.0 all-to-all-done.hid_ref
  41.7 25.4 %all_to_all.25.cot_ref = bf16[8,64,128]{2,1,0:T(8,128)(2,1)S(1)} all-to-all(bf16[8,64,128]{2,1,0:T(8,128)(2,1)S(1)} %broadcast_in_dim.2), channel_id=1, replica_groups=mesh['y'=8,'zh'=2,'x'=4,'zl'=8,'c'=2] {'zl'}, dimensions={0} | all-to-all | bytes 262144 | tf_op jit(solution)/shard_map/all_to_all | solution.py:116
  67.2 0.8 shard_map.85
  68.0 1.9 %collective-permute-start.2 = (bf16[4,8,64,128]{3,2,1,0:T(8,128)(2,1)S(1)}, bf16[4,8,64,128]{3,2,1,0:T(8,128)(2,1)S(1)}, u32[]{:S(2)}, u32[]{:S(2)}) collective-permute-start(bf16[4,8,64,128]{3,2,1,0:T(8,128)(2,1)S(1)} %get-tuple-element.19), channel_id=1, source_target_pairs={{0,1},{1,0},{2,3},{3,2},{4,5},{5,4},{6,7},{7,6},{8,9},{9,8},{10,11... | collective-permute-start | bytes 1572872 | tf_op jit(solution)/shard_map/ppermute | solution.py:142
  69.9 1.9 %collective-permute-done.2.came_ref = bf16[4,8,64,128]{3,2,1,0:T(8,128)(2,1)S(1)} collective-permute-done((bf16[4,8,64,128]{3,2,1,0:T(8,128)(2,1)S(1)}, bf16[4,8,64,128]{3,2,1,0:T(8,128)(2,1)S(1)}, u32[]{:S(2)}, u32[]{:S(2)}) %collective-permute-start.2) | collective-permute-done | bytes 524320 | tf_op jit(solution)/shard_map/ppermute | solution.py:142
  71.8 0.2 shard_map.86
  72.0 17.3 %all_to_all.26.got_ref = bf16[4,16,64,128]{3,2,1,0:T(8,128)(2,1)S(1)} all-to-all(bf16[4,16,64,128]{3,2,1,0:T(8,128)(2,1)S(1)} %shard_map.86), channel_id=1, replica_groups=mesh['y'=8,'zh'=2,'x'=4,'zl'=8,'c'=2] {'x'}, dimensions={0} | all-to-all | bytes 2097152 | tf_op jit(solution)/shard_map/all_to_all | solution.py:148
  89.3 0.7 shard_map.87
  90.0 4.3 %all-to-all-start.3 = ((bf16[8,64,128]{2,1,0:T(8,128)(2,1)}), bf16[8,64,128]{2,1,0:T(8,128)(2,1)S(1)}, u32[]{:S(2)}, u32[]{:S(2)}) async-start(bf16[8,64,128]{2,1,0:T(8,128)(2,1)} %get-tuple-element.20), calls=%async_computation.3 | async-start | bytes 262144 | tf_op jit(solution)/shard_map/all_to_all | solution.py:120
  94.3 1.9 %collective-permute-start.4 = (bf16[4,8,64,128]{3,2,1,0:T(8,128)(2,1)S(1)}, bf16[4,8,64,128]{3,2,1,0:T(8,128)(2,1)S(1)}, u32[]{:S(2)}, u32[]{:S(2)}) collective-permute-start(bf16[4,8,64,128]{3,2,1,0:T(8,128)(2,1)S(1)} %get-tuple-element.21.mine_ref), channel_id=1, source_target_pairs={{0,1},{1,0},{2,3},{3,2},{4,5},{5,4},{6,7},{7,6},{8,9},{9,8},{10,11... | collective-permute-start | bytes 1572872 | tf_op jit(solution)/shard_map/ppermute | solution.py:150
  96.2 9.5 %all-to-all-done.3 = bf16[8,64,128]{2,1,0:T(8,128)(2,1)S(1)} async-done(((bf16[8,64,128]{2,1,0:T(8,128)(2,1)}), bf16[8,64,128]{2,1,0:T(8,128)(2,1)S(1)}, u32[]{:S(2)}, u32[]{:S(2)}) %all-to-all-start.3) | async-done | bytes 131104 | tf_op jit(solution)/shard_map/all_to_all | solution.py:120
  105.8 0.0 collective-permute-done.4.its_ref
  105.8 1.8 %shard_map.88 = (bf16[8,128,256]{2,1,0:T(8,128)(2,1)}, f32[256,256]{1,0:T(8,128)S(1)}, bf16[256,256]{1,0:T(8,128)(2,1)S(1)}) custom-call(bf16[8,128,256]{2,1,0:T(8,128)(2,1)S(1)} %all-to-all-done.hid_ref, bf16[4,8,64,128]{3,2,1,0:T(8,128)(2,1)S(1)} %get-tuple-element.21.mine_ref, bf16[4,8,64,128]{3,2,1,0:T(8,128)(2,1)S(1)} %collective-permute-done.4.its_ref, ...), custom_call_target="tpu_custom_call" | custom-call | flops 536870912 | bytes 2752512 | tf_op jit(solution)/shard_map/pallas_call | solution.py:34
  107.6 0.0 copy-start.5
  107.6 3.6 %all-to-all-start.4 = ((bf16[8,128,256]{2,1,0:T(8,128)(2,1)}), bf16[8,128,256]{2,1,0:T(8,128)(2,1)S(1)}, u32[]{:S(2)}, u32[]{:S(2)}) async-start(bf16[8,128,256]{2,1,0:T(8,128)(2,1)} %get-tuple-element.23), calls=%async_computation.4 | async-start | bytes 1048576 | tf_op jit(solution)/shard_map/all_to_all | solution.py:120
  111.3 9.9 %collective-permute-start.3 = (f32[64,128]{1,0:T(8,128)S(1)}, f32[64,128]{1,0:T(8,128)S(1)}, u32[]{:S(2)}, u32[]{:S(2)}) collective-permute-start(f32[64,128]{1,0:T(8,128)S(1)} %convert_reduce_fusion.1), channel_id=1, source_target_pairs={{0,0},{1,1},{2,2},{3,3},{4,4},{5,5},{6,6},{7,7},{8,128},{9,129},{1... | collective-permute-start | bytes 98312 | tf_op jit(solution)/shard_map/ppermute | solution.py:163
  121.2 9.1 %collective-permute-start.5 = (bf16[256,256]{1,0:T(8,128)(2,1)S(1)}, bf16[256,256]{1,0:T(8,128)(2,1)S(1)}, u32[]{:S(2)}, u32[]{:S(2)}) collective-permute-start(bf16[256,256]{1,0:T(8,128)(2,1)S(1)} %get-tuple-element.25), channel_id=1, source_target_pairs={{0,64},{64,0},{1,65},{65,1},{2,66},{66,2},{3,67},{67,3},{4,68},{68... | collective-permute-start | bytes 393224 | tf_op jit(solution)/shard_map/ppermute | solution.py:164
  130.3 0.0 collective-permute-done.3
  130.3 0.0 copy-done.5
  130.3 0.6 fusion.9
  130.9 11.3 %collective-permute-done.5 = bf16[256,256]{1,0:T(8,128)(2,1)S(1)} collective-permute-done((bf16[256,256]{1,0:T(8,128)(2,1)S(1)}, bf16[256,256]{1,0:T(8,128)(2,1)S(1)}, u32[]{:S(2)}, u32[]{:S(2)}) %collective-permute-start.5) | collective-permute-done | bytes 131104 | tf_op jit(solution)/shard_map/ppermute | solution.py:164
  142.2 0.7 multiply_convert_fusion
  142.9 0.0 copy-start.1
  142.9 0.0 copy-start.3
  142.9 0.0 all-to-all-done.4
  142.9 0.1 convert_reduce_fusion
  143.0 0.8 copy-done.1
  143.8 0.0 copy-done.3
  143.8 0.7 fusion.7
  (2 shorter events, 0.0 us)
Async XLA Ops:
  0.6 0.8 copy-start
  1.5 0.8 copy-start.2
  3.1 7.2 %copy-start.4 = (bf16[256,256]{1,0:T(8,128)(2,1)S(1)}, bf16[256,256]{1,0:T(8,128)(2,1)}, u32[]{:S(2)}) copy-start(bf16[256,256]{1,0:T(8,128)(2,1)} %own_ref.3) | copy-start | bytes 393220
  3.1 26.6 %copy-start.6 = (bf16[128,64]{0,1:T(8,128)(2,1)S(1)}, bf16[128,64]{0,1:T(8,128)(2,1)}, u32[]{:S(2)}) copy-start(bf16[128,64]{0,1:T(8,128)(2,1)} %param.9) | copy-start | bytes 49156
  3.2 38.6 %all-to-all-start = ((bf16[8,128,256]{2,1,0:T(8,128)(2,1)}), bf16[8,128,256]{2,1,0:T(8,128)(2,1)S(1)}, u32[]{:S(2)}, u32[]{:S(2)}) async-start(bf16[8,128,256]{2,1,0:T(8,128)(2,1)} %shard_map.84), calls=%async_computation | async-start | bytes 1048576 | tf_op jit(solution)/shard_map/all_to_all | solution.py:129
  10.4 31.3 %collective-permute-start.1 = (bf16[256,256]{1,0:T(8,128)(2,1)S(1)}, bf16[256,256]{1,0:T(8,128)(2,1)S(1)}, u32[]{:S(2)}, u32[]{:S(2)}) collective-permute-start(bf16[256,256]{1,0:T(8,128)(2,1)S(1)} %copy-done.4), channel_id=1, source_target_pairs={{0,64},{64,0},{1,65},{65,1},{2,66},{66,2},{3,67},{67,3},{4,68},{68... | collective-permute-start | bytes 393224 | tf_op jit(solution)/shard_map/ppermute | solution.py:126
  29.8 11.9 %collective-permute-start = (bf16[64,128]{1,0:T(8,128)(2,1)S(1)}, bf16[64,128]{1,0:T(8,128)(2,1)S(1)}, u32[]{:S(2)}, u32[]{:S(2)}) collective-permute-start(bf16[64,128]{1,0:T(8,128)(2,1)S(1)} %bitcast.9), channel_id=1, source_target_pairs={{0,0},{1,1},{2,2},{3,3},{4,4},{5,5},{6,6},{7,7},{8,128},{9,129},{1... | collective-permute-start | bytes 49160 | tf_op jit(solution)/shard_map/ppermute | solution.py:125
  68.0 3.8 %collective-permute-start.2 = (bf16[4,8,64,128]{3,2,1,0:T(8,128)(2,1)S(1)}, bf16[4,8,64,128]{3,2,1,0:T(8,128)(2,1)S(1)}, u32[]{:S(2)}, u32[]{:S(2)}) collective-permute-start(bf16[4,8,64,128]{3,2,1,0:T(8,128)(2,1)S(1)} %get-tuple-element.19), channel_id=1, source_target_pairs={{0,1},{1,0},{2,3},{3,2},{4,5},{5,4},{6,7},{7,6},{8,9},{9,8},{10,11... | collective-permute-start | bytes 1572872 | tf_op jit(solution)/shard_map/ppermute | solution.py:142
  90.0 15.7 %all-to-all-start.3 = ((bf16[8,64,128]{2,1,0:T(8,128)(2,1)}), bf16[8,64,128]{2,1,0:T(8,128)(2,1)S(1)}, u32[]{:S(2)}, u32[]{:S(2)}) async-start(bf16[8,64,128]{2,1,0:T(8,128)(2,1)} %get-tuple-element.20), calls=%async_computation.3 | async-start | bytes 262144 | tf_op jit(solution)/shard_map/all_to_all | solution.py:120
  94.3 11.5 %collective-permute-start.4 = (bf16[4,8,64,128]{3,2,1,0:T(8,128)(2,1)S(1)}, bf16[4,8,64,128]{3,2,1,0:T(8,128)(2,1)S(1)}, u32[]{:S(2)}, u32[]{:S(2)}) collective-permute-start(bf16[4,8,64,128]{3,2,1,0:T(8,128)(2,1)S(1)} %get-tuple-element.21.mine_ref), channel_id=1, source_target_pairs={{0,1},{1,0},{2,3},{3,2},{4,5},{5,4},{6,7},{7,6},{8,9},{9,8},{10,11... | collective-permute-start | bytes 1572872 | tf_op jit(solution)/shard_map/ppermute | solution.py:150
  107.6 22.7 %copy-start.5 = (bf16[128,64]{0,1:T(8,128)(2,1)S(1)}, bf16[128,64]{0,1:T(8,128)(2,1)}, u32[]{:S(2)}) copy-start(bf16[128,64]{0,1:T(8,128)(2,1)} %param.7) | copy-start | bytes 49156
  107.6 35.3 %all-to-all-start.4 = ((bf16[8,128,256]{2,1,0:T(8,128)(2,1)}), bf16[8,128,256]{2,1,0:T(8,128)(2,1)S(1)}, u32[]{:S(2)}, u32[]{:S(2)}) async-start(bf16[8,128,256]{2,1,0:T(8,128)(2,1)} %get-tuple-element.23), calls=%async_computation.4 | async-start | bytes 1048576 | tf_op jit(solution)/shard_map/all_to_all | solution.py:120
  111.3 19.0 %collective-permute-start.3 = (f32[64,128]{1,0:T(8,128)S(1)}, f32[64,128]{1,0:T(8,128)S(1)}, u32[]{:S(2)}, u32[]{:S(2)}) collective-permute-start(f32[64,128]{1,0:T(8,128)S(1)} %convert_reduce_fusion.1), channel_id=1, source_target_pairs={{0,0},{1,1},{2,2},{3,3},{4,4},{5,5},{6,6},{7,7},{8,128},{9,129},{1... | collective-permute-start | bytes 98312 | tf_op jit(solution)/shard_map/ppermute | solution.py:163
  121.2 21.1 %collective-permute-start.5 = (bf16[256,256]{1,0:T(8,128)(2,1)S(1)}, bf16[256,256]{1,0:T(8,128)(2,1)S(1)}, u32[]{:S(2)}, u32[]{:S(2)}) collective-permute-start(bf16[256,256]{1,0:T(8,128)(2,1)S(1)} %get-tuple-element.25), channel_id=1, source_target_pairs={{0,64},{64,0},{1,65},{65,1},{2,66},{66,2},{3,67},{67,3},{4,68},{68... | collective-permute-start | bytes 393224 | tf_op jit(solution)/shard_map/ppermute | solution.py:164
  142.9 0.8 copy-start.1
  142.9 0.9 copy-start.3

commit v4 on v3

--- a/solution.py
+++ b/solution.py
@@ -125,17 +125,21 @@
     cot_moved = lax.ppermute(cotangent.T, AXES, swap)
     w_other = lax.ppermute(down_proj, "zh", ACROSS)
 
-    (spread,) = in_vmem(hidden_kernel, [shape((8, 128, 256))], 500_000, gate_input, up_input)
+    spread = pl.pallas_call(
+        hidden_kernel,
+        out_shape=shape((8, 128, 256)),
+        cost_estimate=pl.CostEstimate(flops=500_000, bytes_accessed=700_000, transcendentals=0),
+    )(gate_input, up_input)
     hid = lax.all_to_all(spread, "y", 0, 0)
 
-    cot_moved, w_now = lax.optimization_barrier((cot_moved, w_other, hid))[:2]
+    cot_moved, w_now, hid = lax.optimization_barrier((cot_moved, w_other, hid))
     cot_line = gather(cot_moved, "zl")
 
     keep, send = in_vmem(
         proj_kernel,
         [shape((4, 8, 64, 128))] * 2,
         2 * 1024 * 256 * 512,
-        after(hid, cot_line),
+        hid,
         down_proj,
         w_now,
     )
@@ -155,14 +159,14 @@
         4 * 1024 * 256 * 512,
         hid,
         mine,
-        after(its, proj),
+        its,
         down_proj,
         w_now,
         scratch=[pltpu.VMEM((512, 1024), BF)],
     )
     moved = lax.ppermute(proj, AXES, swap)
-    term_in = lax.ppermute(term_out, "zh", ACROSS)
-    hidden_grad = scatter_sum(partial, "y")
+    term_in = lax.ppermute(after(term_out, proj), "zh", ACROSS)
+    hidden_grad = scatter_sum(after(partial, proj), "y")
 
     gate = gate_input.astype(F32)
     up = up_input.astype(F32)

time: 145 us -> 142 us (0.979)
  the two profiles are of different devices: /device:TPU:4 before, /device:TPU:76 now
where the time goes in v4:
time: 142 us
  starting transfers between devices  73.5 us (52%)
  blocking collectives  30.5 us (21%)
  waiting for transfers between devices  28.8 us (20%)
  Pallas kernels  5.28 us (4%)
  other arithmetic  2.11 us (1%)
    ppermute x1, starting transfers between devices, body(): w_other = lax.ppermute(down_proj, 'zh', ACROSS)  18.4 us
    all_to_all x2, starting transfers between devices, scatter_sum(): return jnp.sum(lax.all_to_all(parts, axis, 0, 0).astype(F32), axis=0)  17.6 us
    all_to_all x1, blocking collectives, gather(): lax.all_to_all(jnp.broadcast_to(part[None], (lax.axis_size(axis),) + part...  16.1 us
    ppermute x1, waiting for transfers between devices, body(): term_in = lax.ppermute(after(term_out, proj), 'zh', ACROSS)  14.6 us
    all_to_all x1, blocking collectives, body(): lax.all_to_all(packed, 'x', 0, 0)  14.4 us
    ppermute x1, starting transfers between devices, body(): cot_moved = lax.ppermute(cotangent.T, AXES, swap)  9.96 us
    ppermute x1, starting transfers between devices, body(): moved = lax.ppermute(proj, AXES, swap)  8.54 us
    all_to_all x2, waiting for transfers between devices, scatter_sum(): return jnp.sum(lax.all_to_all(parts, axis, 0, 0).astype(F32), axis=0)  7.73 us
  transfers between devices with their start and end apart: 9, of which 3 were waited for; matrix products, arithmetic and copies ran while one was open for 1% of the time, Pallas kernels for 0%

profile of v4, /device:TPU:76, one launch (start us, length us, event | category | flops | bytes accessed | tf_op | source)
XLA Modules:
  0.0 141.7 jit_solution(10020542924417931448)
XLA Ops:
  0.6 1.7 %shard_map.84 = bf16[8,128,256]{2,1,0:T(8,128)(2,1)} custom-call(bf16[128,256]{1,0:T(8,128)(2,1)} %gate_ref.1, bf16[128,256]{1,0:T(8,128)(2,1)} %up_ref.1), custom_call_target="tpu_custom_call" | custom-call | flops 500000 | bytes 700000 | tf_op jit(solution)/shard_map/pallas_call | solution.py:128
  2.3 0.0 copy-start
  2.3 0.0 copy-start.4
  2.3 7.7 %all-to-all-start = ((bf16[8,128,256]{2,1,0:T(8,128)(2,1)}), bf16[8,128,256]{2,1,0:T(8,128)(2,1)S(1)}, u32[]{:S(2)}, u32[]{:S(2)}) async-start(bf16[8,128,256]{2,1,0:T(8,128)(2,1)} %shard_map.84), calls=%async_computation | async-start | bytes 1048576 | tf_op jit(solution)/shard_map/all_to_all | solution.py:133
  10.0 0.0 copy-done
  10.0 18.4 %collective-permute-start.1 = (bf16[256,256]{1,0:T(8,128)(2,1)S(1)}, bf16[256,256]{1,0:T(8,128)(2,1)S(1)}, u32[]{:S(2)}, u32[]{:S(2)}) collective-permute-start(bf16[256,256]{1,0:T(8,128)(2,1)S(1)} %copy-done), channel_id=1, source_target_pairs={{0,64},{64,0},{1,65},{65,1},{2,66},{66,2},{3,67},{67,3},{4,68},{68... | collective-permute-start | bytes 393224 | tf_op jit(solution)/shard_map/ppermute | solution.py:126
  28.5 0.0 copy-done.4
  28.5 10.0 %collective-permute-start = (bf16[64,128]{1,0:T(8,128)(2,1)S(1)}, bf16[64,128]{1,0:T(8,128)(2,1)S(1)}, u32[]{:S(2)}, u32[]{:S(2)}) collective-permute-start(bf16[64,128]{1,0:T(8,128)(2,1)S(1)} %bitcast.9), channel_id=1, source_target_pairs={{0,0},{1,1},{2,2},{3,3},{4,4},{5,5},{6,6},{7,7},{8,128},{9,129},{1... | collective-permute-start | bytes 49160 | tf_op jit(solution)/shard_map/ppermute | solution.py:125
  38.5 6.5 %collective-permute-done = bf16[64,128]{1,0:T(8,128)(2,1)S(1)} collective-permute-done((bf16[64,128]{1,0:T(8,128)(2,1)S(1)}, bf16[64,128]{1,0:T(8,128)(2,1)S(1)}, u32[]{:S(2)}, u32[]{:S(2)}) %collective-permute-start) | collective-permute-done | bytes 16416 | tf_op jit(solution)/shard_map/ppermute | solution.py:125
  44.9 0.0 collective-permute-done.1.other_ref
  44.9 0.0 all-to-all-done.hid_ref
  45.0 0.8 shard_map.85
  45.8 1.9 %collective-permute-start.2 = (bf16[4,8,64,128]{3,2,1,0:T(8,128)(2,1)S(1)}, bf16[4,8,64,128]{3,2,1,0:T(8,128)(2,1)S(1)}, u32[]{:S(2)}, u32[]{:S(2)}) collective-permute-start(bf16[4,8,64,128]{3,2,1,0:T(8,128)(2,1)S(1)} %get-tuple-element.20), channel_id=1, source_target_pairs={{0,1},{1,0},{2,3},{3,2},{4,5},{5,4},{6,7},{7,6},{8,9},{9,8},{10,11... | collective-permute-start | bytes 1572872 | tf_op jit(solution)/shard_map/ppermute | solution.py:146
  47.7 16.1 %all_to_all.25.cot_ref = bf16[8,64,128]{2,1,0:T(8,128)(2,1)S(1)} all-to-all(bf16[8,64,128]{2,1,0:T(8,128)(2,1)S(1)} %broadcast_in_dim.2), channel_id=1, replica_groups=mesh['y'=8,'zh'=2,'x'=4,'zl'=8,'c'=2] {'zl'}, dimensions={0} | all-to-all | bytes 262144 | tf_op jit(solution)/shard_map/all_to_all | solution.py:116
  63.9 0.0 collective-permute-done.2.came_ref
  63.9 0.2 shard_map.86
  64.0 14.4 %all_to_all.26.got_ref = bf16[4,16,64,128]{3,2,1,0:T(8,128)(2,1)S(1)} all-to-all(bf16[4,16,64,128]{3,2,1,0:T(8,128)(2,1)S(1)} %shard_map.86), channel_id=1, replica_groups=mesh['y'=8,'zh'=2,'x'=4,'zl'=8,'c'=2] {'x'}, dimensions={0} | all-to-all | bytes 2097152 | tf_op jit(solution)/shard_map/all_to_all | solution.py:152
  78.4 0.7 shard_map.87
  79.1 8.0 %all-to-all-start.3 = ((bf16[8,64,128]{2,1,0:T(8,128)(2,1)}), bf16[8,64,128]{2,1,0:T(8,128)(2,1)S(1)}, u32[]{:S(2)}, u32[]{:S(2)}) async-start(bf16[8,64,128]{2,1,0:T(8,128)(2,1)} %get-tuple-element.21), calls=%async_computation.3 | async-start | bytes 262144 | tf_op jit(solution)/shard_map/all_to_all | solution.py:120
  87.1 1.9 %collective-permute-start.4 = (bf16[4,8,64,128]{3,2,1,0:T(8,128)(2,1)S(1)}, bf16[4,8,64,128]{3,2,1,0:T(8,128)(2,1)S(1)}, u32[]{:S(2)}, u32[]{:S(2)}) collective-permute-start(bf16[4,8,64,128]{3,2,1,0:T(8,128)(2,1)S(1)} %get-tuple-element.22.mine_ref), channel_id=1, source_target_pairs={{0,1},{1,0},{2,3},{3,2},{4,5},{5,4},{6,7},{7,6},{8,9},{9,8},{10,11... | collective-permute-start | bytes 1572872 | tf_op jit(solution)/shard_map/ppermute | solution.py:154
  89.1 7.7 %all-to-all-done.3 = bf16[8,64,128]{2,1,0:T(8,128)(2,1)S(1)} async-done(((bf16[8,64,128]{2,1,0:T(8,128)(2,1)}), bf16[8,64,128]{2,1,0:T(8,128)(2,1)S(1)}, u32[]{:S(2)}, u32[]{:S(2)}) %all-to-all-start.3) | async-done | bytes 131104 | tf_op jit(solution)/shard_map/all_to_all | solution.py:120
  96.8 0.0 collective-permute-done.4.its_ref
  96.8 1.8 %shard_map.88 = (bf16[8,128,256]{2,1,0:T(8,128)(2,1)}, f32[256,256]{1,0:T(8,128)S(1)}, bf16[256,256]{1,0:T(8,128)(2,1)S(1)}) custom-call(bf16[8,128,256]{2,1,0:T(8,128)(2,1)S(1)} %all-to-all-done.hid_ref, bf16[4,8,64,128]{3,2,1,0:T(8,128)(2,1)S(1)} %get-tuple-element.22.mine_ref, bf16[4,8,64,128]{3,2,1,0:T(8,128)(2,1)S(1)} %collective-permute-done.4.its_ref, ...), custom_call_target="tpu_custom_call" | custom-call | flops 536870912 | bytes 2752512 | tf_op jit(solution)/shard_map/pallas_call | solution.py:34
  98.7 0.0 copy-start.3
  98.7 9.6 %all-to-all-start.4 = ((bf16[8,128,256]{2,1,0:T(8,128)(2,1)}), bf16[8,128,256]{2,1,0:T(8,128)(2,1)S(1)}, u32[]{:S(2)}, u32[]{:S(2)}) async-start(bf16[8,128,256]{2,1,0:T(8,128)(2,1)} %get-tuple-element.24), calls=%async_computation.4 | async-start | bytes 1048576 | tf_op jit(solution)/shard_map/all_to_all | solution.py:120
  108.2 8.5 %collective-permute-start.3 = (f32[64,128]{1,0:T(8,128)S(1)}, f32[64,128]{1,0:T(8,128)S(1)}, u32[]{:S(2)}, u32[]{:S(2)}) collective-permute-start(f32[64,128]{1,0:T(8,128)S(1)} %convert_reduce_fusion.1), channel_id=1, source_target_pairs={{0,0},{1,1},{2,2},{3,3},{4,4},{5,5},{6,6},{7,7},{8,128},{9,129},{1... | collective-permute-start | bytes 98312 | tf_op jit(solution)/shard_map/ppermute | solution.py:167
  116.8 7.5 %collective-permute-start.5 = (bf16[256,256]{1,0:T(8,128)(2,1)S(1)}, bf16[256,256]{1,0:T(8,128)(2,1)S(1)}, u32[]{:S(2)}, u32[]{:S(2)}) collective-permute-start(bf16[256,256]{1,0:T(8,128)(2,1)S(1)} %get-tuple-element.27), channel_id=1, source_target_pairs={{0,64},{64,0},{1,65},{65,1},{2,66},{66,2},{3,67},{67,3},{4,68},{68... | collective-permute-start | bytes 393224 | tf_op jit(solution)/shard_map/ppermute | solution.py:168
  124.2 0.0 collective-permute-done.3
  124.3 0.0 copy-done.3
  124.3 0.6 fusion.9
  124.9 14.6 %collective-permute-done.5 = bf16[256,256]{1,0:T(8,128)(2,1)S(1)} collective-permute-done((bf16[256,256]{1,0:T(8,128)(2,1)S(1)}, bf16[256,256]{1,0:T(8,128)(2,1)S(1)}, u32[]{:S(2)}, u32[]{:S(2)}) %collective-permute-start.5) | collective-permute-done | bytes 131104 | tf_op jit(solution)/shard_map/ppermute | solution.py:168
  139.4 0.7 multiply_convert_fusion
  140.1 0.0 copy-start.1
  140.1 0.0 copy-start.2
  140.1 0.0 all-to-all-done.4
  140.1 0.1 convert_reduce_fusion
  140.2 0.8 copy-done.1
  141.0 0.0 copy-done.2
  141.0 0.7 fusion.7
  (2 shorter events, 0.0 us)
Async XLA Ops:
  2.3 7.7 %copy-start = (bf16[256,256]{1,0:T(8,128)(2,1)S(1)}, bf16[256,256]{1,0:T(8,128)(2,1)}, u32[]{:S(2)}) copy-start(bf16[256,256]{1,0:T(8,128)(2,1)} %own_ref.3) | copy-start | bytes 393220
  2.3 26.1 %copy-start.4 = (bf16[128,64]{0,1:T(8,128)(2,1)S(1)}, bf16[128,64]{0,1:T(8,128)(2,1)}, u32[]{:S(2)}) copy-start(bf16[128,64]{0,1:T(8,128)(2,1)} %param.9) | copy-start | bytes 49156
  2.3 42.6 %all-to-all-start = ((bf16[8,128,256]{2,1,0:T(8,128)(2,1)}), bf16[8,128,256]{2,1,0:T(8,128)(2,1)S(1)}, u32[]{:S(2)}, u32[]{:S(2)}) async-start(bf16[8,128,256]{2,1,0:T(8,128)(2,1)} %shard_map.84), calls=%async_computation | async-start | bytes 1048576 | tf_op jit(solution)/shard_map/all_to_all | solution.py:133
  10.0 34.9 %collective-permute-start.1 = (bf16[256,256]{1,0:T(8,128)(2,1)S(1)}, bf16[256,256]{1,0:T(8,128)(2,1)S(1)}, u32[]{:S(2)}, u32[]{:S(2)}) collective-permute-start(bf16[256,256]{1,0:T(8,128)(2,1)S(1)} %copy-done), channel_id=1, source_target_pairs={{0,64},{64,0},{1,65},{65,1},{2,66},{66,2},{3,67},{67,3},{4,68},{68... | collective-permute-start | bytes 393224 | tf_op jit(solution)/shard_map/ppermute | solution.py:126
  28.5 16.5 %collective-permute-start = (bf16[64,128]{1,0:T(8,128)(2,1)S(1)}, bf16[64,128]{1,0:T(8,128)(2,1)S(1)}, u32[]{:S(2)}, u32[]{:S(2)}) collective-permute-start(bf16[64,128]{1,0:T(8,128)(2,1)S(1)} %bitcast.9), channel_id=1, source_target_pairs={{0,0},{1,1},{2,2},{3,3},{4,4},{5,5},{6,6},{7,7},{8,128},{9,129},{1... | collective-permute-start | bytes 49160 | tf_op jit(solution)/shard_map/ppermute | solution.py:125
  45.8 18.1 %collective-permute-start.2 = (bf16[4,8,64,128]{3,2,1,0:T(8,128)(2,1)S(1)}, bf16[4,8,64,128]{3,2,1,0:T(8,128)(2,1)S(1)}, u32[]{:S(2)}, u32[]{:S(2)}) collective-permute-start(bf16[4,8,64,128]{3,2,1,0:T(8,128)(2,1)S(1)} %get-tuple-element.20), channel_id=1, source_target_pairs={{0,1},{1,0},{2,3},{3,2},{4,5},{5,4},{6,7},{7,6},{8,9},{9,8},{10,11... | collective-permute-start | bytes 1572872 | tf_op jit(solution)/shard_map/ppermute | solution.py:146
  79.1 17.7 %all-to-all-start.3 = ((bf16[8,64,128]{2,1,0:T(8,128)(2,1)}), bf16[8,64,128]{2,1,0:T(8,128)(2,1)S(1)}, u32[]{:S(2)}, u32[]{:S(2)}) async-start(bf16[8,64,128]{2,1,0:T(8,128)(2,1)} %get-tuple-element.21), calls=%async_computation.3 | async-start | bytes 262144 | tf_op jit(solution)/shard_map/all_to_all | solution.py:120
  87.1 9.7 %collective-permute-start.4 = (bf16[4,8,64,128]{3,2,1,0:T(8,128)(2,1)S(1)}, bf16[4,8,64,128]{3,2,1,0:T(8,128)(2,1)S(1)}, u32[]{:S(2)}, u32[]{:S(2)}) collective-permute-start(bf16[4,8,64,128]{3,2,1,0:T(8,128)(2,1)S(1)} %get-tuple-element.22.mine_ref), channel_id=1, source_target_pairs={{0,1},{1,0},{2,3},{3,2},{4,5},{5,4},{6,7},{7,6},{8,9},{9,8},{10,11... | collective-permute-start | bytes 1572872 | tf_op jit(solution)/shard_map/ppermute | solution.py:154
  98.7 25.6 %copy-start.3 = (bf16[128,64]{0,1:T(8,128)(2,1)S(1)}, bf16[128,64]{0,1:T(8,128)(2,1)}, u32[]{:S(2)}) copy-start(bf16[128,64]{0,1:T(8,128)(2,1)} %param.7) | copy-start | bytes 49156
  98.7 41.5 %all-to-all-start.4 = ((bf16[8,128,256]{2,1,0:T(8,128)(2,1)}), bf16[8,128,256]{2,1,0:T(8,128)(2,1)S(1)}, u32[]{:S(2)}, u32[]{:S(2)}) async-start(bf16[8,128,256]{2,1,0:T(8,128)(2,1)} %get-tuple-element.24), calls=%async_computation.4 | async-start | bytes 1048576 | tf_op jit(solution)/shard_map/all_to_all | solution.py:120
  108.2 16.0 %collective-permute-start.3 = (f32[64,128]{1,0:T(8,128)S(1)}, f32[64,128]{1,0:T(8,128)S(1)}, u32[]{:S(2)}, u32[]{:S(2)}) collective-permute-start(f32[64,128]{1,0:T(8,128)S(1)} %convert_reduce_fusion.1), channel_id=1, source_target_pairs={{0,0},{1,1},{2,2},{3,3},{4,4},{5,5},{6,6},{7,7},{8,128},{9,129},{1... | collective-permute-start | bytes 98312 | tf_op jit(solution)/shard_map/ppermute | solution.py:167
  116.8 22.7 %collective-permute-start.5 = (bf16[256,256]{1,0:T(8,128)(2,1)S(1)}, bf16[256,256]{1,0:T(8,128)(2,1)S(1)}, u32[]{:S(2)}, u32[]{:S(2)}) collective-permute-start(bf16[256,256]{1,0:T(8,128)(2,1)S(1)} %get-tuple-element.27), channel_id=1, source_target_pairs={{0,64},{64,0},{1,65},{65,1},{2,66},{66,2},{3,67},{67,3},{4,68},{68... | collective-permute-start | bytes 393224 | tf_op jit(solution)/shard_map/ppermute | solution.py:168
  140.1 0.8 copy-start.1
  140.1 0.9 copy-start.2

commit v5 on v4

--- a/solution.py
+++ b/solution.py
@@ -132,9 +132,7 @@
     )(gate_input, up_input)
     hid = lax.all_to_all(spread, "y", 0, 0)
 
-    cot_moved, w_now, hid = lax.optimization_barrier((cot_moved, w_other, hid))
-    cot_line = gather(cot_moved, "zl")
-
+    w_now = w_other
     keep, send = in_vmem(
         proj_kernel,
         [shape((4, 8, 64, 128))] * 2,
@@ -143,7 +141,10 @@
         down_proj,
         w_now,
     )
+    send, cot_moved = lax.optimization_barrier((send, cot_moved))
     came = lax.ppermute(send, "c", ACROSS)
+    cot_line = gather(cot_moved, "zl")
+
     (packed,) = in_vmem(pack_kernel, [shape((4, 16, 64, 128))], 300_000, cot_line, keep, came)
     mine, proj = in_vmem(
         unpack_kernel,
@@ -173,8 +174,8 @@
     sig = jax.nn.sigmoid(gate)
     up_grad = (hidden_grad * gate * sig).astype(BF)
     gate_grad = (hidden_grad * up * sig * (1.0 + gate * (1.0 - sig))).astype(BF)
-    layer_out = (residual.astype(F32).T + moved).astype(BF).T
     down_grad = ((term + term_in.astype(F32)) * (1.0 / math.sqrt(2048))).astype(BF)
+    layer_out = (after(residual, down_grad).astype(F32).T + moved).astype(BF).T
     return (layer_out, gate_grad, up_grad, down_grad)
 
 

time: 142 us -> 140 us (0.986)
  the two profiles are of different devices: /device:TPU:76 before, /device:TPU:12 now
where the time goes in v5:
time: 140 us; the launch traced here: 139 us
  starting transfers between devices  73 us (52%)
  blocking collectives  30.8 us (22%)
  waiting for transfers between devices  26.7 us (19%)
  Pallas kernels  5.28 us (4%)
  other arithmetic  2.11 us (2%)
    ppermute x1, starting transfers between devices, body(): w_other = lax.ppermute(down_proj, 'zh', ACROSS)  19.3 us
    all_to_all x1, blocking collectives, body(): lax.all_to_all(packed, 'x', 0, 0)  15.6 us
    all_to_all x2, starting transfers between devices, scatter_sum(): return jnp.sum(lax.all_to_all(parts, axis, 0, 0).astype(F32), axis=0)  15.3 us
    all_to_all x1, blocking collectives, gather(): lax.all_to_all(jnp.broadcast_to(part[None], (lax.axis_size(axis),) + part...  15.3 us
    ppermute x1, starting transfers between devices, body(): cot_moved = lax.ppermute(cotangent.T, AXES, swap)  9.96 us
    all_to_all x2, waiting for transfers between devices, scatter_sum(): return jnp.sum(lax.all_to_all(parts, axis, 0, 0).astype(F32), axis=0)  9.54 us
    ppermute x1, starting transfers between devices, body(): term_in = lax.ppermute(after(term_out, proj), 'zh', ACROSS)  8.51 us
    ppermute x1, starting transfers between devices, body(): moved = lax.ppermute(proj, AXES, swap)  8.36 us
  transfers between devices with their start and end apart: 9, of which 4 were waited for; matrix products, arithmetic and copies ran while one was open for 1% of the time, Pallas kernels for 1%

profile of v5, /device:TPU:12, one launch (start us, length us, event | category | flops | bytes accessed | tf_op | source)
XLA Modules:
  0.0 139.5 jit_solution(2376742102770831596)
XLA Ops:
  0.6 1.7 %shard_map.84 = bf16[8,128,256]{2,1,0:T(8,128)(2,1)} custom-call(bf16[128,256]{1,0:T(8,128)(2,1)} %gate_ref.1, bf16[128,256]{1,0:T(8,128)(2,1)} %up_ref.1), custom_call_target="tpu_custom_call" | custom-call | flops 500000 | bytes 700000 | tf_op jit(solution)/shard_map/pallas_call | solution.py:128
  2.3 0.0 copy-start
  2.3 0.0 copy-start.4
  2.3 7.7 %all-to-all-start = ((bf16[8,128,256]{2,1,0:T(8,128)(2,1)}), bf16[8,128,256]{2,1,0:T(8,128)(2,1)S(1)}, u32[]{:S(2)}, u32[]{:S(2)}) async-start(bf16[8,128,256]{2,1,0:T(8,128)(2,1)} %shard_map.84), calls=%async_computation | async-start | bytes 1048576 | tf_op jit(solution)/shard_map/all_to_all | solution.py:133
  10.0 0.0 copy-done
  10.0 19.3 %collective-permute-start = (bf16[256,256]{1,0:T(8,128)(2,1)S(1)}, bf16[256,256]{1,0:T(8,128)(2,1)S(1)}, u32[]{:S(2)}, u32[]{:S(2)}) collective-permute-start(bf16[256,256]{1,0:T(8,128)(2,1)S(1)} %copy-done), channel_id=1, source_target_pairs={{0,64},{64,0},{1,65},{65,1},{2,66},{66,2},{3,67},{67,3},{4,68},{68... | collective-permute-start | bytes 393224 | tf_op jit(solution)/shard_map/ppermute | solution.py:126
  29.4 0.0 copy-done.4
  29.4 10.0 %collective-permute-start.1 = (bf16[64,128]{1,0:T(8,128)(2,1)S(1)}, bf16[64,128]{1,0:T(8,128)(2,1)S(1)}, u32[]{:S(2)}, u32[]{:S(2)}) collective-permute-start(bf16[64,128]{1,0:T(8,128)(2,1)S(1)} %bitcast.9), channel_id=1, source_target_pairs={{0,0},{1,1},{2,2},{3,3},{4,4},{5,5},{6,6},{7,7},{8,128},{9,129},{1... | collective-permute-start | bytes 49160 | tf_op jit(solution)/shard_map/ppermute | solution.py:125
  39.4 0.0 collective-permute-done.other_ref
  39.4 0.0 all-to-all-done.hid_ref
  39.4 0.8 shard_map.85
  40.2 6.9 %collective-permute-done.1 = bf16[64,128]{1,0:T(8,128)(2,1)S(1)} collective-permute-done((bf16[64,128]{1,0:T(8,128)(2,1)S(1)}, bf16[64,128]{1,0:T(8,128)(2,1)S(1)}, u32[]{:S(2)}, u32[]{:S(2)}) %collective-permute-start.1) | collective-permute-done | bytes 16416 | tf_op jit(solution)/shard_map/ppermute | solution.py:125
  47.1 1.9 %collective-permute-start.2 = (bf16[4,8,64,128]{3,2,1,0:T(8,128)(2,1)S(1)}, bf16[4,8,64,128]{3,2,1,0:T(8,128)(2,1)S(1)}, u32[]{:S(2)}, u32[]{:S(2)}) collective-permute-start(bf16[4,8,64,128]{3,2,1,0:T(8,128)(2,1)S(1)} %get-tuple-element.19), channel_id=1, source_target_pairs={{0,1},{1,0},{2,3},{3,2},{4,5},{5,4},{6,7},{7,6},{8,9},{9,8},{10,11... | collective-permute-start | bytes 1572872 | tf_op jit(solution)/shard_map/ppermute | solution.py:145
  49.0 15.3 %all_to_all.25.cot_ref = bf16[8,64,128]{2,1,0:T(8,128)(2,1)S(1)} all-to-all(bf16[8,64,128]{2,1,0:T(8,128)(2,1)S(1)} %broadcast_in_dim.2), channel_id=1, replica_groups=mesh['y'=8,'zh'=2,'x'=4,'zl'=8,'c'=2] {'zl'}, dimensions={0} | all-to-all | bytes 262144 | tf_op jit(solution)/shard_map/all_to_all | solution.py:116
  64.3 0.0 collective-permute-done.2.came_ref
  64.3 0.2 shard_map.86
  64.5 15.6 %all_to_all.26.got_ref = bf16[4,16,64,128]{3,2,1,0:T(8,128)(2,1)S(1)} all-to-all(bf16[4,16,64,128]{3,2,1,0:T(8,128)(2,1)S(1)} %shard_map.86), channel_id=1, replica_groups=mesh['y'=8,'zh'=2,'x'=4,'zl'=8,'c'=2] {'x'}, dimensions={0} | all-to-all | bytes 2097152 | tf_op jit(solution)/shard_map/all_to_all | solution.py:153
  80.0 0.7 shard_map.87
  80.8 5.9 %all-to-all-start.3 = ((bf16[8,64,128]{2,1,0:T(8,128)(2,1)}), bf16[8,64,128]{2,1,0:T(8,128)(2,1)S(1)}, u32[]{:S(2)}, u32[]{:S(2)}) async-start(bf16[8,64,128]{2,1,0:T(8,128)(2,1)} %get-tuple-element.23), calls=%async_computation.3 | async-start | bytes 262144 | tf_op jit(solution)/shard_map/all_to_all | solution.py:120
  86.6 1.9 %collective-permute-start.3 = (bf16[4,8,64,128]{3,2,1,0:T(8,128)(2,1)S(1)}, bf16[4,8,64,128]{3,2,1,0:T(8,128)(2,1)S(1)}, u32[]{:S(2)}, u32[]{:S(2)}) collective-permute-start(bf16[4,8,64,128]{3,2,1,0:T(8,128)(2,1)S(1)} %get-tuple-element.20.mine_ref), channel_id=1, source_target_pairs={{0,1},{1,0},{2,3},{3,2},{4,5},{5,4},{6,7},{7,6},{8,9},{9,8},{10,11... | collective-permute-start | bytes 1572872 | tf_op jit(solution)/shard_map/ppermute | solution.py:155
  88.5 9.5 %all-to-all-done.3 = bf16[8,64,128]{2,1,0:T(8,128)(2,1)S(1)} async-done(((bf16[8,64,128]{2,1,0:T(8,128)(2,1)}), bf16[8,64,128]{2,1,0:T(8,128)(2,1)S(1)}, u32[]{:S(2)}, u32[]{:S(2)}) %all-to-all-start.3) | async-done | bytes 131104 | tf_op jit(solution)/shard_map/all_to_all | solution.py:120
  98.1 0.0 collective-permute-done.3.its_ref
  98.1 1.8 %shard_map.88 = (bf16[8,128,256]{2,1,0:T(8,128)(2,1)}, f32[256,256]{1,0:T(8,128)S(1)}, bf16[256,256]{1,0:T(8,128)(2,1)S(1)}) custom-call(bf16[8,128,256]{2,1,0:T(8,128)(2,1)S(1)} %all-to-all-done.hid_ref, bf16[4,8,64,128]{3,2,1,0:T(8,128)(2,1)S(1)} %get-tuple-element.20.mine_ref, bf16[4,8,64,128]{3,2,1,0:T(8,128)(2,1)S(1)} %collective-permute-done.3.its_ref, ...), custom_call_target="tpu_custom_call" | custom-call | flops 536870912 | bytes 2752512 | tf_op jit(solution)/shard_map/pallas_call | solution.py:34
  100.0 9.4 %all-to-all-start.4 = ((bf16[8,128,256]{2,1,0:T(8,128)(2,1)}), bf16[8,128,256]{2,1,0:T(8,128)(2,1)S(1)}, u32[]{:S(2)}, u32[]{:S(2)}) async-start(bf16[8,128,256]{2,1,0:T(8,128)(2,1)} %get-tuple-element.27), calls=%async_computation.4 | async-start | bytes 1048576 | tf_op jit(solution)/shard_map/all_to_all | solution.py:120
  109.4 8.5 %collective-permute-start.4 = (bf16[256,256]{1,0:T(8,128)(2,1)S(1)}, bf16[256,256]{1,0:T(8,128)(2,1)S(1)}, u32[]{:S(2)}, u32[]{:S(2)}) collective-permute-start(bf16[256,256]{1,0:T(8,128)(2,1)S(1)} %get-tuple-element.24), channel_id=1, source_target_pairs={{0,64},{64,0},{1,65},{65,1},{2,66},{66,2},{3,67},{67,3},{4,68},{68... | collective-permute-start | bytes 393224 | tf_op jit(solution)/shard_map/ppermute | solution.py:169
  117.9 8.4 %collective-permute-start.5 = (f32[64,128]{1,0:T(8,128)S(1)}, f32[64,128]{1,0:T(8,128)S(1)}, u32[]{:S(2)}, u32[]{:S(2)}) collective-permute-start(f32[64,128]{1,0:T(8,128)S(1)} %convert_reduce_fusion.1), channel_id=1, source_target_pairs={{0,0},{1,1},{2,2},{3,3},{4,4},{5,5},{6,6},{7,7},{8,128},{9,129},{1... | collective-permute-start | bytes 98312 | tf_op jit(solution)/shard_map/ppermute | solution.py:168
  126.3 4.6 %collective-permute-done.4 = bf16[256,256]{1,0:T(8,128)(2,1)S(1)} collective-permute-done((bf16[256,256]{1,0:T(8,128)(2,1)S(1)}, bf16[256,256]{1,0:T(8,128)(2,1)S(1)}, u32[]{:S(2)}, u32[]{:S(2)}) %collective-permute-start.4) | collective-permute-done | bytes 131104 | tf_op jit(solution)/shard_map/ppermute | solution.py:169
  130.9 0.0 copy-start.3
  130.9 0.7 multiply_convert_fusion
  131.6 5.7 %collective-permute-done.5 = f32[64,128]{1,0:T(8,128)S(1)} collective-permute-done((f32[64,128]{1,0:T(8,128)S(1)}, f32[64,128]{1,0:T(8,128)S(1)}, u32[]{:S(2)}, u32[]{:S(2)}) %collective-permute-start.5) | collective-permute-done | bytes 32800 | tf_op jit(solution)/shard_map/ppermute | solution.py:168
  137.3 0.0 copy-done.3
  137.3 0.6 fusion.9
  137.9 0.0 copy-start.1
  137.9 0.0 copy-start.2
  137.9 0.0 all-to-all-done.4
  137.9 0.1 convert_reduce_fusion
  138.0 0.8 copy-done.1
  138.7 0.0 copy-done.2
  138.8 0.7 fusion.7
  (2 shorter events, 0.0 us)
Async XLA Ops:
  2.3 7.7 %copy-start = (bf16[256,256]{1,0:T(8,128)(2,1)S(1)}, bf16[256,256]{1,0:T(8,128)(2,1)}, u32[]{:S(2)}) copy-start(bf16[256,256]{1,0:T(8,128)(2,1)} %own_ref.3) | copy-start | bytes 393220
  2.3 27.0 %copy-start.4 = (bf16[128,64]{0,1:T(8,128)(2,1)S(1)}, bf16[128,64]{0,1:T(8,128)(2,1)}, u32[]{:S(2)}) copy-start(bf16[128,64]{0,1:T(8,128)(2,1)} %param.9) | copy-start | bytes 49156
  2.3 37.0 %all-to-all-start = ((bf16[8,128,256]{2,1,0:T(8,128)(2,1)}), bf16[8,128,256]{2,1,0:T(8,128)(2,1)S(1)}, u32[]{:S(2)}, u32[]{:S(2)}) async-start(bf16[8,128,256]{2,1,0:T(8,128)(2,1)} %shard_map.84), calls=%async_computation | async-start | bytes 1048576 | tf_op jit(solution)/shard_map/all_to_all | solution.py:133
  10.0 29.3 %collective-permute-start = (bf16[256,256]{1,0:T(8,128)(2,1)S(1)}, bf16[256,256]{1,0:T(8,128)(2,1)S(1)}, u32[]{:S(2)}, u32[]{:S(2)}) collective-permute-start(bf16[256,256]{1,0:T(8,128)(2,1)S(1)} %copy-done), channel_id=1, source_target_pairs={{0,64},{64,0},{1,65},{65,1},{2,66},{66,2},{3,67},{67,3},{4,68},{68... | collective-permute-start | bytes 393224 | tf_op jit(solution)/shard_map/ppermute | solution.py:126
  29.4 17.7 %collective-permute-start.1 = (bf16[64,128]{1,0:T(8,128)(2,1)S(1)}, bf16[64,128]{1,0:T(8,128)(2,1)S(1)}, u32[]{:S(2)}, u32[]{:S(2)}) collective-permute-start(bf16[64,128]{1,0:T(8,128)(2,1)S(1)} %bitcast.9), channel_id=1, source_target_pairs={{0,0},{1,1},{2,2},{3,3},{4,4},{5,5},{6,6},{7,7},{8,128},{9,129},{1... | collective-permute-start | bytes 49160 | tf_op jit(solution)/shard_map/ppermute | solution.py:125
  47.1 17.2 %collective-permute-start.2 = (bf16[4,8,64,128]{3,2,1,0:T(8,128)(2,1)S(1)}, bf16[4,8,64,128]{3,2,1,0:T(8,128)(2,1)S(1)}, u32[]{:S(2)}, u32[]{:S(2)}) collective-permute-start(bf16[4,8,64,128]{3,2,1,0:T(8,128)(2,1)S(1)} %get-tuple-element.19), channel_id=1, source_target_pairs={{0,1},{1,0},{2,3},{3,2},{4,5},{5,4},{6,7},{7,6},{8,9},{9,8},{10,11... | collective-permute-start | bytes 1572872 | tf_op jit(solution)/shard_map/ppermute | solution.py:145
  80.8 17.3 %all-to-all-start.3 = ((bf16[8,64,128]{2,1,0:T(8,128)(2,1)}), bf16[8,64,128]{2,1,0:T(8,128)(2,1)S(1)}, u32[]{:S(2)}, u32[]{:S(2)}) async-start(bf16[8,64,128]{2,1,0:T(8,128)(2,1)} %get-tuple-element.23), calls=%async_computation.3 | async-start | bytes 262144 | tf_op jit(solution)/shard_map/all_to_all | solution.py:120
  86.6 11.5 %collective-permute-start.3 = (bf16[4,8,64,128]{3,2,1,0:T(8,128)(2,1)S(1)}, bf16[4,8,64,128]{3,2,1,0:T(8,128)(2,1)S(1)}, u32[]{:S(2)}, u32[]{:S(2)}) collective-permute-start(bf16[4,8,64,128]{3,2,1,0:T(8,128)(2,1)S(1)} %get-tuple-element.20.mine_ref), channel_id=1, source_target_pairs={{0,1},{1,0},{2,3},{3,2},{4,5},{5,4},{6,7},{7,6},{8,9},{9,8},{10,11... | collective-permute-start | bytes 1572872 | tf_op jit(solution)/shard_map/ppermute | solution.py:155
  100.0 38.0 %all-to-all-start.4 = ((bf16[8,128,256]{2,1,0:T(8,128)(2,1)}), bf16[8,128,256]{2,1,0:T(8,128)(2,1)S(1)}, u32[]{:S(2)}, u32[]{:S(2)}) async-start(bf16[8,128,256]{2,1,0:T(8,128)(2,1)} %get-tuple-element.27), calls=%async_computation.4 | async-start | bytes 1048576 | tf_op jit(solution)/shard_map/all_to_all | solution.py:120
  109.4 21.5 %collective-permute-start.4 = (bf16[256,256]{1,0:T(8,128)(2,1)S(1)}, bf16[256,256]{1,0:T(8,128)(2,1)S(1)}, u32[]{:S(2)}, u32[]{:S(2)}) collective-permute-start(bf16[256,256]{1,0:T(8,128)(2,1)S(1)} %get-tuple-element.24), channel_id=1, source_target_pairs={{0,64},{64,0},{1,65},{65,1},{2,66},{66,2},{3,67},{67,3},{4,68},{68... | collective-permute-start | bytes 393224 | tf_op jit(solution)/shard_map/ppermute | solution.py:169
  117.9 19.4 %collective-permute-start.5 = (f32[64,128]{1,0:T(8,128)S(1)}, f32[64,128]{1,0:T(8,128)S(1)}, u32[]{:S(2)}, u32[]{:S(2)}) collective-permute-start(f32[64,128]{1,0:T(8,128)S(1)} %convert_reduce_fusion.1), channel_id=1, source_target_pairs={{0,0},{1,1},{2,2},{3,3},{4,4},{5,5},{6,6},{7,7},{8,128},{9,129},{1... | collective-permute-start | bytes 98312 | tf_op jit(solution)/shard_map/ppermute | solution.py:168
  130.9 6.4 %copy-start.3 = (bf16[128,64]{0,1:T(8,128)(2,1)S(1)}, bf16[128,64]{0,1:T(8,128)(2,1)}, u32[]{:S(2)}) copy-start(bf16[128,64]{0,1:T(8,128)(2,1)} %param.7) | copy-start | bytes 49156
  137.9 0.8 copy-start.1
  137.9 0.9 copy-start.2

commit v6 on v5

--- a/solution.py
+++ b/solution.py
@@ -175,7 +175,7 @@
     up_grad = (hidden_grad * gate * sig).astype(BF)
     gate_grad = (hidden_grad * up * sig * (1.0 + gate * (1.0 - sig))).astype(BF)
     down_grad = ((term + term_in.astype(F32)) * (1.0 / math.sqrt(2048))).astype(BF)
-    layer_out = (after(residual, down_grad).astype(F32).T + moved).astype(BF).T
+    layer_out = (after(residual, down_grad, up_grad).astype(F32).T + moved).astype(BF).T
     return (layer_out, gate_grad, up_grad, down_grad)
 
 

time: 140 us -> 139 us (level)
  waiting for transfers between devices: 26.7 us -> 25.1 us
    ppermute x1, waiting for transfers between devices: 5.67 us -> 4.08 us  [body(): moved = lax.ppermute(proj, AXES, swap)]
where the time goes in v6:
time: 139 us; the launch traced here: 138 us
  starting transfers between devices  73 us (53%)
  blocking collectives  30.8 us (22%)
  waiting for transfers between devices  25.1 us (18%)
  Pallas kernels  5.28 us (4%)
  other arithmetic  2.11 us (2%)
    ppermute x1, starting transfers between devices, body(): w_other = lax.ppermute(down_proj, 'zh', ACROSS)  19.3 us
    all_to_all x1, blocking collectives, body(): lax.all_to_all(packed, 'x', 0, 0)  15.6 us
    all_to_all x2, starting transfers between devices, scatter_sum(): return jnp.sum(lax.all_to_all(parts, axis, 0, 0).astype(F32), axis=0)  15.3 us
    all_to_all x1, blocking collectives, gather(): lax.all_to_all(jnp.broadcast_to(part[None], (lax.axis_size(axis),) + part...  15.3 us
    ppermute x1, starting transfers between devices, body(): cot_moved = lax.ppermute(cotangent.T, AXES, swap)  9.96 us
    all_to_all x2, waiting for transfers between devices, scatter_sum(): return jnp.sum(lax.all_to_all(parts, axis, 0, 0).astype(F32), axis=0)  9.54 us
    ppermute x1, starting transfers between devices, body(): term_in = lax.ppermute(after(term_out, proj), 'zh', ACROSS)  8.51 us
    ppermute x1, starting transfers between devices, body(): moved = lax.ppermute(proj, AXES, swap)  8.36 us
  transfers between devices with their start and end apart: 9, of which 4 were waited for; matrix products, arithmetic and copies ran while one was open for 1% of the time, Pallas kernels for 1%

profile of v6, /device:TPU:12, one launch (start us, length us, event | category | flops | bytes accessed | tf_op | source)
XLA Modules:
  0.0 137.9 jit_solution(6704987812955503049)
XLA Ops:
  0.6 1.7 %shard_map.84 = bf16[8,128,256]{2,1,0:T(8,128)(2,1)} custom-call(bf16[128,256]{1,0:T(8,128)(2,1)} %gate_ref.1, bf16[128,256]{1,0:T(8,128)(2,1)} %up_ref.1), custom_call_target="tpu_custom_call" | custom-call | flops 500000 | bytes 700000 | tf_op jit(solution)/shard_map/pallas_call | solution.py:128
  2.3 0.0 copy-start
  2.3 0.0 copy-start.4
  2.3 7.7 %all-to-all-start = ((bf16[8,128,256]{2,1,0:T(8,128)(2,1)}), bf16[8,128,256]{2,1,0:T(8,128)(2,1)S(1)}, u32[]{:S(2)}, u32[]{:S(2)}) async-start(bf16[8,128,256]{2,1,0:T(8,128)(2,1)} %shard_map.84), calls=%async_computation | async-start | bytes 1048576 | tf_op jit(solution)/shard_map/all_to_all | solution.py:133
  10.0 0.0 copy-done
  10.0 19.3 %collective-permute-start = (bf16[256,256]{1,0:T(8,128)(2,1)S(1)}, bf16[256,256]{1,0:T(8,128)(2,1)S(1)}, u32[]{:S(2)}, u32[]{:S(2)}) collective-permute-start(bf16[256,256]{1,0:T(8,128)(2,1)S(1)} %copy-done), channel_id=1, source_target_pairs={{0,64},{64,0},{1,65},{65,1},{2,66},{66,2},{3,67},{67,3},{4,68},{68... | collective-permute-start | bytes 393224 | tf_op jit(solution)/shard_map/ppermute | solution.py:126
  29.4 0.0 copy-done.4
  29.4 10.0 %collective-permute-start.1 = (bf16[64,128]{1,0:T(8,128)(2,1)S(1)}, bf16[64,128]{1,0:T(8,128)(2,1)S(1)}, u32[]{:S(2)}, u32[]{:S(2)}) collective-permute-start(bf16[64,128]{1,0:T(8,128)(2,1)S(1)} %bitcast.9), channel_id=1, source_target_pairs={{0,0},{1,1},{2,2},{3,3},{4,4},{5,5},{6,6},{7,7},{8,128},{9,129},{1... | collective-permute-start | bytes 49160 | tf_op jit(solution)/shard_map/ppermute | solution.py:125
  39.4 0.0 collective-permute-done.other_ref
  39.4 0.0 all-to-all-done.hid_ref
  39.4 0.8 shard_map.85
  40.2 6.9 %collective-permute-done.1 = bf16[64,128]{1,0:T(8,128)(2,1)S(1)} collective-permute-done((bf16[64,128]{1,0:T(8,128)(2,1)S(1)}, bf16[64,128]{1,0:T(8,128)(2,1)S(1)}, u32[]{:S(2)}, u32[]{:S(2)}) %collective-permute-start.1) | collective-permute-done | bytes 16416 | tf_op jit(solution)/shard_map/ppermute | solution.py:125
  47.1 1.9 %collective-permute-start.2 = (bf16[4,8,64,128]{3,2,1,0:T(8,128)(2,1)S(1)}, bf16[4,8,64,128]{3,2,1,0:T(8,128)(2,1)S(1)}, u32[]{:S(2)}, u32[]{:S(2)}) collective-permute-start(bf16[4,8,64,128]{3,2,1,0:T(8,128)(2,1)S(1)} %get-tuple-element.19), channel_id=1, source_target_pairs={{0,1},{1,0},{2,3},{3,2},{4,5},{5,4},{6,7},{7,6},{8,9},{9,8},{10,11... | collective-permute-start | bytes 1572872 | tf_op jit(solution)/shard_map/ppermute | solution.py:145
  49.0 15.3 %all_to_all.25.cot_ref = bf16[8,64,128]{2,1,0:T(8,128)(2,1)S(1)} all-to-all(bf16[8,64,128]{2,1,0:T(8,128)(2,1)S(1)} %broadcast_in_dim.2), channel_id=1, replica_groups=mesh['y'=8,'zh'=2,'x'=4,'zl'=8,'c'=2] {'zl'}, dimensions={0} | all-to-all | bytes 262144 | tf_op jit(solution)/shard_map/all_to_all | solution.py:116
  64.3 0.0 collective-permute-done.2.came_ref
  64.3 0.2 shard_map.86
  64.5 15.6 %all_to_all.26.got_ref = bf16[4,16,64,128]{3,2,1,0:T(8,128)(2,1)S(1)} all-to-all(bf16[4,16,64,128]{3,2,1,0:T(8,128)(2,1)S(1)} %shard_map.86), channel_id=1, replica_groups=mesh['y'=8,'zh'=2,'x'=4,'zl'=8,'c'=2] {'x'}, dimensions={0} | all-to-all | bytes 2097152 | tf_op jit(solution)/shard_map/all_to_all | solution.py:153
  80.0 0.7 shard_map.87
  80.8 5.9 %all-to-all-start.3 = ((bf16[8,64,128]{2,1,0:T(8,128)(2,1)}), bf16[8,64,128]{2,1,0:T(8,128)(2,1)S(1)}, u32[]{:S(2)}, u32[]{:S(2)}) async-start(bf16[8,64,128]{2,1,0:T(8,128)(2,1)} %get-tuple-element.23), calls=%async_computation.3 | async-start | bytes 262144 | tf_op jit(solution)/shard_map/all_to_all | solution.py:120
  86.6 1.9 %collective-permute-start.3 = (bf16[4,8,64,128]{3,2,1,0:T(8,128)(2,1)S(1)}, bf16[4,8,64,128]{3,2,1,0:T(8,128)(2,1)S(1)}, u32[]{:S(2)}, u32[]{:S(2)}) collective-permute-start(bf16[4,8,64,128]{3,2,1,0:T(8,128)(2,1)S(1)} %get-tuple-element.20.mine_ref), channel_id=1, source_target_pairs={{0,1},{1,0},{2,3},{3,2},{4,5},{5,4},{6,7},{7,6},{8,9},{9,8},{10,11... | collective-permute-start | bytes 1572872 | tf_op jit(solution)/shard_map/ppermute | solution.py:155
  88.5 9.5 %all-to-all-done.3 = bf16[8,64,128]{2,1,0:T(8,128)(2,1)S(1)} async-done(((bf16[8,64,128]{2,1,0:T(8,128)(2,1)}), bf16[8,64,128]{2,1,0:T(8,128)(2,1)S(1)}, u32[]{:S(2)}, u32[]{:S(2)}) %all-to-all-start.3) | async-done | bytes 131104 | tf_op jit(solution)/shard_map/all_to_all | solution.py:120
  98.1 0.0 collective-permute-done.3.its_ref
  98.1 1.8 %shard_map.88 = (bf16[8,128,256]{2,1,0:T(8,128)(2,1)}, f32[256,256]{1,0:T(8,128)S(1)}, bf16[256,256]{1,0:T(8,128)(2,1)S(1)}) custom-call(bf16[8,128,256]{2,1,0:T(8,128)(2,1)S(1)} %all-to-all-done.hid_ref, bf16[4,8,64,128]{3,2,1,0:T(8,128)(2,1)S(1)} %get-tuple-element.20.mine_ref, bf16[4,8,64,128]{3,2,1,0:T(8,128)(2,1)S(1)} %collective-permute-done.3.its_ref, ...), custom_call_target="tpu_custom_call" | custom-call | flops 536870912 | bytes 2752512 | tf_op jit(solution)/shard_map/pallas_call | solution.py:34
  100.0 9.4 %all-to-all-start.4 = ((bf16[8,128,256]{2,1,0:T(8,128)(2,1)}), bf16[8,128,256]{2,1,0:T(8,128)(2,1)S(1)}, u32[]{:S(2)}, u32[]{:S(2)}) async-start(bf16[8,128,256]{2,1,0:T(8,128)(2,1)} %get-tuple-element.26), calls=%async_computation.4 | async-start | bytes 1048576 | tf_op jit(solution)/shard_map/all_to_all | solution.py:120
  109.4 8.5 %collective-permute-start.4 = (bf16[256,256]{1,0:T(8,128)(2,1)S(1)}, bf16[256,256]{1,0:T(8,128)(2,1)S(1)}, u32[]{:S(2)}, u32[]{:S(2)}) collective-permute-start(bf16[256,256]{1,0:T(8,128)(2,1)S(1)} %get-tuple-element.24), channel_id=1, source_target_pairs={{0,64},{64,0},{1,65},{65,1},{2,66},{66,2},{3,67},{67,3},{4,68},{68... | collective-permute-start | bytes 393224 | tf_op jit(solution)/shard_map/ppermute | solution.py:169
  117.9 8.4 %collective-permute-start.5 = (f32[64,128]{1,0:T(8,128)S(1)}, f32[64,128]{1,0:T(8,128)S(1)}, u32[]{:S(2)}, u32[]{:S(2)}) collective-permute-start(f32[64,128]{1,0:T(8,128)S(1)} %convert_reduce_fusion.1), channel_id=1, source_target_pairs={{0,0},{1,1},{2,2},{3,3},{4,4},{5,5},{6,6},{7,7},{8,128},{9,129},{1... | collective-permute-start | bytes 98312 | tf_op jit(solution)/shard_map/ppermute | solution.py:168
  126.3 4.6 %collective-permute-done.4 = bf16[256,256]{1,0:T(8,128)(2,1)S(1)} collective-permute-done((bf16[256,256]{1,0:T(8,128)(2,1)S(1)}, bf16[256,256]{1,0:T(8,128)(2,1)S(1)}, u32[]{:S(2)}, u32[]{:S(2)}) %collective-permute-start.4) | collective-permute-done | bytes 131104 | tf_op jit(solution)/shard_map/ppermute | solution.py:169
  130.9 0.7 multiply_convert_fusion
  131.6 0.0 copy-start.1
  131.6 0.0 copy-start.2
  131.6 0.0 all-to-all-done.4
  131.6 0.1 convert_reduce_fusion
  131.7 0.8 copy-done.1
  132.5 0.0 copy-done.2
  132.5 0.0 copy-start.3
  132.5 0.7 fusion.7
  133.2 4.1 %collective-permute-done.5 = f32[64,128]{1,0:T(8,128)S(1)} collective-permute-done((f32[64,128]{1,0:T(8,128)S(1)}, f32[64,128]{1,0:T(8,128)S(1)}, u32[]{:S(2)}, u32[]{:S(2)}) %collective-permute-start.5) | collective-permute-done | bytes 32800 | tf_op jit(solution)/shard_map/ppermute | solution.py:168
  137.3 0.0 copy-done.3
  137.3 0.6 fusion.9
  (2 shorter events, 0.0 us)
Async XLA Ops:
  2.3 7.7 %copy-start = (bf16[256,256]{1,0:T(8,128)(2,1)S(1)}, bf16[256,256]{1,0:T(8,128)(2,1)}, u32[]{:S(2)}) copy-start(bf16[256,256]{1,0:T(8,128)(2,1)} %own_ref.3) | copy-start | bytes 393220
  2.3 27.0 %copy-start.4 = (bf16[128,64]{0,1:T(8,128)(2,1)S(1)}, bf16[128,64]{0,1:T(8,128)(2,1)}, u32[]{:S(2)}) copy-start(bf16[128,64]{0,1:T(8,128)(2,1)} %param.9) | copy-start | bytes 49156
  2.3 37.0 %all-to-all-start = ((bf16[8,128,256]{2,1,0:T(8,128)(2,1)}), bf16[8,128,256]{2,1,0:T(8,128)(2,1)S(1)}, u32[]{:S(2)}, u32[]{:S(2)}) async-start(bf16[8,128,256]{2,1,0:T(8,128)(2,1)} %shard_map.84), calls=%async_computation | async-start | bytes 1048576 | tf_op jit(solution)/shard_map/all_to_all | solution.py:133
  10.0 29.3 %collective-permute-start = (bf16[256,256]{1,0:T(8,128)(2,1)S(1)}, bf16[256,256]{1,0:T(8,128)(2,1)S(1)}, u32[]{:S(2)}, u32[]{:S(2)}) collective-permute-start(bf16[256,256]{1,0:T(8,128)(2,1)S(1)} %copy-done), channel_id=1, source_target_pairs={{0,64},{64,0},{1,65},{65,1},{2,66},{66,2},{3,67},{67,3},{4,68},{68... | collective-permute-start | bytes 393224 | tf_op jit(solution)/shard_map/ppermute | solution.py:126
  29.4 17.7 %collective-permute-start.1 = (bf16[64,128]{1,0:T(8,128)(2,1)S(1)}, bf16[64,128]{1,0:T(8,128)(2,1)S(1)}, u32[]{:S(2)}, u32[]{:S(2)}) collective-permute-start(bf16[64,128]{1,0:T(8,128)(2,1)S(1)} %bitcast.9), channel_id=1, source_target_pairs={{0,0},{1,1},{2,2},{3,3},{4,4},{5,5},{6,6},{7,7},{8,128},{9,129},{1... | collective-permute-start | bytes 49160 | tf_op jit(solution)/shard_map/ppermute | solution.py:125
  47.1 17.2 %collective-permute-start.2 = (bf16[4,8,64,128]{3,2,1,0:T(8,128)(2,1)S(1)}, bf16[4,8,64,128]{3,2,1,0:T(8,128)(2,1)S(1)}, u32[]{:S(2)}, u32[]{:S(2)}) collective-permute-start(bf16[4,8,64,128]{3,2,1,0:T(8,128)(2,1)S(1)} %get-tuple-element.19), channel_id=1, source_target_pairs={{0,1},{1,0},{2,3},{3,2},{4,5},{5,4},{6,7},{7,6},{8,9},{9,8},{10,11... | collective-permute-start | bytes 1572872 | tf_op jit(solution)/shard_map/ppermute | solution.py:145
  80.8 17.3 %all-to-all-start.3 = ((bf16[8,64,128]{2,1,0:T(8,128)(2,1)}), bf16[8,64,128]{2,1,0:T(8,128)(2,1)S(1)}, u32[]{:S(2)}, u32[]{:S(2)}) async-start(bf16[8,64,128]{2,1,0:T(8,128)(2,1)} %get-tuple-element.23), calls=%async_computation.3 | async-start | bytes 262144 | tf_op jit(solution)/shard_map/all_to_all | solution.py:120
  86.6 11.5 %collective-permute-start.3 = (bf16[4,8,64,128]{3,2,1,0:T(8,128)(2,1)S(1)}, bf16[4,8,64,128]{3,2,1,0:T(8,128)(2,1)S(1)}, u32[]{:S(2)}, u32[]{:S(2)}) collective-permute-start(bf16[4,8,64,128]{3,2,1,0:T(8,128)(2,1)S(1)} %get-tuple-element.20.mine_ref), channel_id=1, source_target_pairs={{0,1},{1,0},{2,3},{3,2},{4,5},{5,4},{6,7},{7,6},{8,9},{9,8},{10,11... | collective-permute-start | bytes 1572872 | tf_op jit(solution)/shard_map/ppermute | solution.py:155
  100.0 31.7 %all-to-all-start.4 = ((bf16[8,128,256]{2,1,0:T(8,128)(2,1)}), bf16[8,128,256]{2,1,0:T(8,128)(2,1)S(1)}, u32[]{:S(2)}, u32[]{:S(2)}) async-start(bf16[8,128,256]{2,1,0:T(8,128)(2,1)} %get-tuple-element.26), calls=%async_computation.4 | async-start | bytes 1048576 | tf_op jit(solution)/shard_map/all_to_all | solution.py:120
  109.4 21.5 %collective-permute-start.4 = (bf16[256,256]{1,0:T(8,128)(2,1)S(1)}, bf16[256,256]{1,0:T(8,128)(2,1)S(1)}, u32[]{:S(2)}, u32[]{:S(2)}) collective-permute-start(bf16[256,256]{1,0:T(8,128)(2,1)S(1)} %get-tuple-element.24), channel_id=1, source_target_pairs={{0,64},{64,0},{1,65},{65,1},{2,66},{66,2},{3,67},{67,3},{4,68},{68... | collective-permute-start | bytes 393224 | tf_op jit(solution)/shard_map/ppermute | solution.py:169
  117.9 19.4 %collective-permute-start.5 = (f32[64,128]{1,0:T(8,128)S(1)}, f32[64,128]{1,0:T(8,128)S(1)}, u32[]{:S(2)}, u32[]{:S(2)}) collective-permute-start(f32[64,128]{1,0:T(8,128)S(1)} %convert_reduce_fusion.1), channel_id=1, source_target_pairs={{0,0},{1,1},{2,2},{3,3},{4,4},{5,5},{6,6},{7,7},{8,128},{9,129},{1... | collective-permute-start | bytes 98312 | tf_op jit(solution)/shard_map/ppermute | solution.py:168
  131.6 0.8 copy-start.1
  131.6 0.9 copy-start.2
  132.5 4.8 %copy-start.3 = (bf16[128,64]{0,1:T(8,128)(2,1)S(1)}, bf16[128,64]{0,1:T(8,128)(2,1)}, u32[]{:S(2)}) copy-start(bf16[128,64]{0,1:T(8,128)(2,1)} %param.7) | copy-start | bytes 49156
